TPU v7x, 256 devices: a whole 4x4x8 slice. The times are simulated.
256 devices in a mesh: seq: 32 (over y, z), chan: 8 (over x, core).
Axes of the slice: x: 4, y: 4, z: 8, core: 2. Of those that a mesh axis runs over, the one named last changes fastest.
Arguments:
- q_branch: bfloat16 [4096, 8192], P('seq', 'chan'), may hold values from -6 to 6
- k_branch: bfloat16 [4096, 8192], P('seq', 'chan'), may hold values from -6 to 6
- v_branch: bfloat16 [4096, 8192], P('seq', 'chan'), may hold values from -6 to 6
- filter_taps: float32 [8192, 2048], P('chan', 'seq'), may hold values from -1 to 1, as said below
- out_weight: bfloat16 [8192, 8192], P('seq', 'chan'), may hold values from -0.0625 to 0.0625
- lengths: int32 [8], replicated, may hold values from 1 to 2048, 4096 in all
Outputs:
- block_output: bfloat16 [4096, 8192], P('seq', 'chan')
Inputs may be any that keep to these rules, and one draw needn't show every extreme that they name: The 8 lengths add up to 4096; the longest is exactly 2048. `filter_taps`: real filter taps.
All inputs are finite; a program needn't handle non-finite values.
Results may differ from a plain program's by a relative error of at most 0.0064.
Values may be sent and summed in bfloat16 or wider, within the bound.
A program may use at most 128 MiB of HBM per device.

v0:
```python
import math

import jax
import jax.numpy as jnp
from jax import lax
from jax.sharding import PartitionSpec as P

dft_precision = lax.Precision.HIGH


def record_tables(lengths, total, slot):
    offsets = jnp.cumsum(lengths) - lengths
    positions = jnp.arange(slot, dtype=jnp.int32)
    live = positions[None, :] < lengths[:, None]
    source = jnp.where(live, offsets[:, None] + positions[None, :], 0).reshape(-1)
    tokens = jnp.arange(total, dtype=jnp.int32)
    started = offsets[None, :] <= tokens[:, None]
    record = jnp.sum(started.astype(jnp.int32), axis=1) - 1
    begin = jnp.max(jnp.where(started, offsets[None, :], 0), axis=1)
    target = record * slot + tokens - begin
    return (source, live.reshape(-1), target)


def angle_table(rows, cols, period):
    grid = (
        jnp.arange(rows, dtype=jnp.int32)[:, None]
        * jnp.arange(cols, dtype=jnp.int32)[None, :]
        % period
    )
    angles = grid.astype(jnp.float32) * (2.0 * math.pi / period)
    return (jnp.cos(angles), jnp.sin(angles))


def dft_tables(count_a, count_b):
    cos_a, sin_a = angle_table(count_a, count_a // 2, count_a)
    cos_t, sin_t = angle_table(count_a, count_b, count_a * count_b)
    cos_b, sin_b = angle_table(count_b, count_b, count_b)
    return (cos_a, sin_a, cos_t, sin_t, cos_b, sin_b)


def matmul_last(left, right):
    return jnp.einsum("bkm,mj->bkj", left, right, precision=dft_precision)


def forward_dft(signal, tables):
    cos_a, sin_a, cos_t, sin_t, cos_b, sin_b = tables
    first_re = jnp.einsum("kn,bnm->bkm", cos_a, signal, precision=dft_precision)
    first_im = -jnp.einsum("kn,bnm->bkm", sin_a, signal, precision=dft_precision)
    turned_re = first_re * cos_t + first_im * sin_t
    turned_im = first_im * cos_t - first_re * sin_t
    out_re = matmul_last(turned_re, cos_b) + matmul_last(turned_im, sin_b)
    out_im = matmul_last(turned_im, cos_b) - matmul_last(turned_re, sin_b)
    return (out_re, out_im)


def inverse_dft(spec_re, spec_im, tables):
    cos_a, sin_a, cos_t, sin_t, cos_b, sin_b = tables
    back_re = matmul_last(spec_re, cos_b) - matmul_last(spec_im, sin_b)
    back_im = matmul_last(spec_im, cos_b) + matmul_last(spec_re, sin_b)
    turned_re = back_re * cos_t - back_im * sin_t
    turned_im = back_im * cos_t + back_re * sin_t
    result = jnp.einsum("kn,bkm->bnm", cos_a, turned_re, precision=dft_precision)
    result = result - jnp.einsum("kn,bkm->bnm", sin_a, turned_im, precision=dft_precision)
    return result / float(cos_t.shape[0] * cos_t.shape[1])


def shards(q_branch, k_branch, v_branch, filter_taps, out_weight, lengths):
    groups = lax.axis_size("seq")
    product = (k_branch.astype(jnp.float32) * v_branch.astype(jnp.float32)).astype(jnp.bfloat16)
    local_rows = q_branch.shape[0]
    total = local_rows * groups
    slot = filter_taps.shape[1] * groups
    records = lengths.shape[0]
    response_taps = lax.all_to_all(filter_taps, "seq", split_axis=0, concat_axis=1, tiled=True)
    stream, gate_cols = (
        lax.all_to_all(product.T, "seq", split_axis=0, concat_axis=1, tiled=True),
        lax.all_to_all(q_branch.T, "seq", split_axis=0, concat_axis=1, tiled=True),
    )
    channels = stream.shape[0]
    source, live, target = record_tables(lengths, total, slot)
    picked = jnp.take(stream, source, axis=1).astype(jnp.float32)
    slotted = jnp.where(live[None, :], picked, jnp.float32(0.0))
    count_b = 128
    count_a = 2 * slot // count_b
    half = count_a // 2
    tables = dft_tables(count_a, count_b)
    signal_re, signal_im = forward_dft(slotted.reshape(channels * records, half, count_b), tables)
    filter_re, filter_im = forward_dft(response_taps.reshape(channels, half, count_b), tables)
    signal_re = signal_re.reshape(channels, records, count_a, count_b)
    signal_im = signal_im.reshape(channels, records, count_a, count_b)
    filter_re = filter_re[:, None]
    filter_im = filter_im[:, None]
    spec_re = (signal_re * filter_re - signal_im * filter_im).reshape(
        channels * records, count_a, count_b
    )
    spec_im = (signal_re * filter_im + signal_im * filter_re).reshape(
        channels * records, count_a, count_b
    )
    convolved = inverse_dft(spec_re, spec_im, tables).reshape(channels, records * slot)
    conv_sent = jnp.take(convolved, target, axis=1).astype(jnp.bfloat16)
    gated_cols = (gate_cols.astype(jnp.float32) * conv_sent.astype(jnp.float32)).astype(
        jnp.bfloat16
    )
    gated = lax.all_to_all(gated_cols, "seq", split_axis=1, concat_axis=0, tiled=True).T
    features = lax.all_gather(gated, "chan", axis=1, tiled=True)
    projected = jnp.dot(
        features,
        lax.all_gather(out_weight, "seq", axis=0, tiled=True),
        preferred_element_type=jnp.float32,
    )
    return projected.astype(jnp.bfloat16)


def solution(mesh):
    in_specs = (
        P("seq", "chan"),
        P("seq", "chan"),
        P("seq", "chan"),
        P("chan", "seq"),
        P("seq", "chan"),
        P(),
    )
    out_specs = P("seq", "chan")
    return jax.shard_map(shards, mesh=mesh, in_specs=in_specs, out_specs=out_specs, check_vma=False)
```

profile of v0, /device:TPU:1, one launch (start us, length us, event | category | flops | bytes accessed | tf_op | source)
XLA Modules:
  0.0 384.8 jit_solution(14741482469793579855)
XLA Ops:
  6.5 1.2 copy.47
  7.7 1.0 reshape.270
  8.8 12.0 %all-to-all-start.2 = ((f32[32,1,2048]{2,1,0:T(1,128)}), f32[32,1,2048]{2,1,0:T(1,128)S(1)}, u32[]{:S(2)}, u32[]{:S(2)}) async-start(f32[32,1,2048]{2,1,0:T(1,128)} %reshape.270), calls=%async_computation.2 | async-start | bytes 524288 | tf_op jit(solution)/shard_map/all_to_all | solution.py:74
  20.8 0.8 reduce-window.9
  21.6 0.7 bitcast_subtract_fusion.1
  22.3 0.8 compare_and_fusion
  23.1 0.7 select_bitcast_fusion
  23.8 0.2 convert_reduce_fusion
  24.0 0.1 copy.65
  24.0 0.1 compare_select_fusion
  24.1 1.1 copy.41
  25.3 1.1 copy.42
  26.5 0.8 multiply_convert_fusion
  27.2 0.1 fusion.108
  27.3 0.8 copy.40
  28.2 2.3 all-to-all-done.2
  30.5 6.9 %all-to-all-start.1 = ((bf16[32,32,128]{2,1,0:T(8,128)(2,1)}), bf16[32,32,128]{2,1,0:T(8,128)(2,1)S(1)}, u32[]{:S(2)}, u32[]{:S(2)}) async-start(bf16[32,32,128]{2,1,0:T(8,128)(2,1)} %bitcast.10), calls=%async_computation.1 | async-start | bytes 524288 | tf_op jit(solution)/shard_map/all_to_all | solution.py:76
  37.4 0.5 broadcast.298
  38.0 1.2 reduce
  39.2 0.2 reshape.271
  39.4 0.3 copy.48
  39.7 0.1 reshape.248
  39.9 0.5 convolution_negate_fusion
  40.4 0.5 fusion.103
  40.8 1.4 fusion.54
  42.3 1.4 fusion.50
  43.7 3.4 all-to-all-done.1
  47.1 6.2 %all-to-all-start = ((bf16[32,32,128]{2,1,0:T(8,128)(2,1)}), bf16[32,32,128]{2,1,0:T(8,128)(2,1)S(1)}, u32[]{:S(2)}, u32[]{:S(2)}) async-start(bf16[32,32,128]{2,1,0:T(8,128)(2,1)} %bitcast.1), calls=%async_computation | async-start | bytes 524288 | tf_op jit(solution)/shard_map/all_to_all | solution.py:77
  53.3 0.0 all-gather.3.cloned.1.call-start
  53.4 0.5 copy.43
  53.8 57.8 %gather_fusion = bf16[16384,32]{1,0:T(8,128)(2,1)} fusion(bf16[32,4096]{0,1:T(8,128)(2,1)S(1)} %bitcast.138, s32[16384]{0:T(1024)S(1)} %broadcast_clamp_fusion), kind=kCustom, calls=%fused_computation | custom fusion | bytes 2162688 | tf_op jit(solution)/shard_map/jit(_take)/gather | solution.py:81
  111.7 3.5 copy.44
  115.1 0.7 gather.13
  115.8 0.1 bitcast_select_fusion
  116.0 0.2 broadcast_in_dim.53
  116.2 2.0 fusion.44
  118.2 2.9 fusion.2
  121.2 4.2 %fusion.20 = f32[256,32,128]{2,0,1:T(8,128)S(1)} fusion(f32[256,32,128]{2,1,0:T(8,128)S(1)} %get-tuple-element.10), kind=kOutput, calls=%fused_computation.30 | convolution fusion | flops 805535744 | bytes 8388608 | tf_op jit(solution)/shard_map/bkm,mj->bkj/dot_general | solution.py:42
  125.4 4.4 %fusion.22 = f32[256,32,128]{2,0,1:T(8,128)S(1)} fusion(f32[256,32,128]{2,1,0:T(8,128)S(1)} %get-tuple-element.10), kind=kOutput, calls=%fused_computation.32 | convolution fusion | flops 805535744 | bytes 8388608 | tf_op jit(solution)/shard_map/bkm,mj->bkj/dot_general | solution.py:42
  129.8 0.6 convolution_add_fusion
  130.4 0.3 copy.49
  130.8 0.6 convolution_subtract_fusion
  131.4 0.3 copy.52
  131.7 4.3 %fusion.31 = f32[256,32,128]{2,0,1:T(8,128)S(1)} fusion(f32[256,32,128]{2,0,1:T(8,128)S(1)} %fusion.20, f32[256,32,128]{2,1,0:T(8,128)S(1)} %get-tuple-element.9), kind=kOutput, calls=%fused_computation.39 | convolution fusion | flops 806584320 | bytes 12582912 | tf_op jit(solution)/shard_map/bkm,mj->bkj/dot_general | solution.py:42
  136.0 5.5 %fusion = (f32[256,32,128]{2,0,1:T(8,128)S(1)}, f32[256,32,128]{2,0,1:T(8,128)S(1)}) fusion(f32[256,32,128]{2,0,1:T(8,128)S(1)} %fusion.31, f32[32,32,128]{2,0,1:T(8,128)S(1)} %copy.52, f32[32,32,128]{2,0,1:T(8,128)S(1)} %copy.49, f32[256,32,128]{2,0,1:T(8,128)S(1)} %fusion.22, f32[256,32,128]{2,1,0:T(8,128)S(1)} %get-tuple-element.9), kind=kOutput, calls=%fused_computation.6 | convolution fusion | flops 812875776 | bytes 22020096 | tf_op jit(solution)/shard_map/bkm,mj->bkj/dot_general | solution.py:42
  141.5 4.1 %fusion.12 = f32[256,32,128]{2,1,0:T(8,128)S(1)} fusion(f32[256,32,128]{2,0,1:T(8,128)S(1)} %get-tuple-element.8), kind=kOutput, calls=%fused_computation.22 | convolution fusion | flops 805535744 | bytes 8388608 | tf_op jit(solution)/shard_map/bkm,mj->bkj/dot_general | solution.py:42
  145.6 4.2 %fusion.14 = f32[256,32,128]{2,1,0:T(8,128)S(1)} fusion(f32[256,32,128]{2,0,1:T(8,128)S(1)} %get-tuple-element.8), kind=kOutput, calls=%fused_computation.24 | convolution fusion | flops 805535744 | bytes 8388608 | tf_op jit(solution)/shard_map/bkm,mj->bkj/dot_general | solution.py:42
  149.8 4.3 %fusion.37 = f32[256,32,128]{2,1,0:T(8,128)S(1)} fusion(f32[256,32,128]{2,1,0:T(8,128)S(1)} %fusion.12, f32[256,32,128]{2,0,1:T(8,128)S(1)} %get-tuple-element.7), kind=kOutput, calls=%fused_computation.41 | convolution fusion | flops 806584320 | bytes 12582912 | tf_op jit(solution)/shard_map/bkm,mj->bkj/dot_general | solution.py:42
  154.2 4.2 %fusion.34 = f32[256,32,128]{2,1,0:T(8,128)S(1)} fusion(f32[256,32,128]{2,1,0:T(8,128)S(1)} %fusion.14, f32[256,32,128]{2,0,1:T(8,128)S(1)} %get-tuple-element.7), kind=kOutput, calls=%fused_computation.40 | convolution fusion | flops 806584320 | bytes 12582912 | tf_op jit(solution)/shard_map/bkm,mj->bkj/dot_general | solution.py:42
  158.4 1.5 fusion.4
  159.9 1.6 multiply_bitcast_fusion
  161.5 0.5 reshape.249
  162.0 3.1 copy.57
  165.1 13.7 %gather_fusion.1 = bf16[4096,32]{1,0:T(8,128)(2,1)S(1)} fusion(bf16[32,16384]{0,1:T(8,128)(2,1)} %copy.57, s32[4096]{0:T(1024)S(1)} %broadcast_clamp_fusion.1), kind=kCustom, calls=%fused_computation.1 | custom fusion | bytes 540672 | tf_op jit(solution)/shard_map/jit(_take)/gather | solution.py:100
  178.9 0.3 copy.58
  179.2 0.0 all-to-all-done
  179.3 0.1 fusion.56
  179.4 18.8 %all_to_all.64 = bf16[32,32,128]{2,0,1:T(8,128)(2,1)} all-to-all(bf16[32,32,128]{2,0,1:T(8,128)(2,1)S(1)} %fusion.56), channel_id=1, replica_groups=mesh['seq'=32,'chan'=8] {'seq'}, dimensions={1} | all-to-all | bytes 524288 | tf_op jit(solution)/shard_map/all_to_all | solution.py:104
  198.2 0.0 all-gather.3.cloned.1.call-update
  198.2 0.3 all-gather.5.cloned.1.call-start
  198.4 0.5 all-gather.5.cloned.1.call-update
  198.9 26.6 %all-gather.3.cloned.1.call-done = bf16[128,8192]{0,1:T(8,128)(2,1)} async-done(((bf16[128,1024]{0,1:T(8,128)(2,1)}), bf16[128,8192]{0,1:T(8,128)(2,1)}) %all-gather.3.cloned.1.call-update) | async-done | bytes 2097168 | tf_op jit(solution)/shard_map/all_gather | solution.py:105
  225.6 142.7 %all-gather.5.cloned.1.call-done = bf16[8192,1024]{1,0:T(8,128)(2,1)} async-done(((bf16[256,1024]{1,0:T(8,128)(2,1)}), bf16[8192,1024]{1,0:T(8,128)(2,1)}) %all-gather.5.cloned.1.call-update) | async-done | bytes 16777232 | tf_op jit(solution)/shard_map/all_gather | solution.py:108
  368.3 9.5 %convolution_convert_fusion = bf16[128,1024]{1,0:T(8,128)(2,1)} fusion(bf16[128,8192]{0,1:T(8,128)(2,1)} %all-gather.3.cloned.1.call-done, bf16[8192,1024]{1,0:T(8,128)(2,1)} %all-gather.5.cloned.1.call-done), kind=kOutput, calls=%fused_computation.54 | convolution fusion | flops 2147614720 | bytes 19136512 | tf_op jit(solution)/shard_map/dot_general | solution.py:106
  (11 shorter events, 0.1 us)
Async XLA Ops:
  6.5 20.8 %copy-start.2 = (bf16[128,1024]{1,0:T(8,128)(2,1)S(1)}, bf16[128,1024]{1,0:T(8,128)(2,1)}, u32[]{:S(2)}) copy-start(bf16[128,1024]{1,0:T(8,128)(2,1)} %param.6) | copy-start | bytes 786436
  8.8 21.7 %all-to-all-start.2 = ((f32[32,1,2048]{2,1,0:T(1,128)}), f32[32,1,2048]{2,1,0:T(1,128)S(1)}, u32[]{:S(2)}, u32[]{:S(2)}) async-start(f32[32,1,2048]{2,1,0:T(1,128)} %reshape.270), calls=%async_computation.2 | async-start | bytes 524288 | tf_op jit(solution)/shard_map/all_to_all | solution.py:74
  30.5 16.6 %all-to-all-start.1 = ((bf16[32,32,128]{2,1,0:T(8,128)(2,1)}), bf16[32,32,128]{2,1,0:T(8,128)(2,1)S(1)}, u32[]{:S(2)}, u32[]{:S(2)}) async-start(bf16[32,32,128]{2,1,0:T(8,128)(2,1)} %bitcast.10), calls=%async_computation.1 | async-start | bytes 524288 | tf_op jit(solution)/shard_map/all_to_all | solution.py:76
  47.1 132.1 %all-to-all-start = ((bf16[32,32,128]{2,1,0:T(8,128)(2,1)}), bf16[32,32,128]{2,1,0:T(8,128)(2,1)S(1)}, u32[]{:S(2)}, u32[]{:S(2)}) async-start(bf16[32,32,128]{2,1,0:T(8,128)(2,1)} %bitcast.1), calls=%async_computation | async-start | bytes 524288 | tf_op jit(solution)/shard_map/all_to_all | solution.py:77
  53.3 172.3 %all-gather.3.cloned.1.call-start = ((), (), s32[]{:S(2)}) async-start(), calls=%async_computation.4 | async-start | bytes 2359296 | tf_op jit(solution)/shard_map/all_gather | solution.py:105
  125.4 4.4 %copy-start.1 = (f32[32,32,128]{2,1,0:T(8,128)S(1)}, f32[32,32,128]{2,1,0:T(8,128)}, u32[]{:S(2)}) copy-start(f32[32,32,128]{2,1,0:T(8,128)} %fusion.54) | copy-start | bytes 1572868
  125.4 5.4 %copy-start = (f32[32,32,128]{2,1,0:T(8,128)S(1)}, f32[32,32,128]{2,1,0:T(8,128)}, u32[]{:S(2)}) copy-start(f32[32,32,128]{2,1,0:T(8,128)} %fusion.50) | copy-start | bytes 1572868
  198.2 170.1 %all-gather.5.cloned.1.call-start = ((), (), s32[]{:S(2)}) async-start(), calls=%async_computation.5 | async-start | bytes 17301504 | tf_op jit(solution)/shard_map/all_gather | solution.py:108
Sparse Core Ops, SparseCore 0:
  198.3 27.2 all-gather.2
  228.2 140.1 all-gather.4
where the time goes:
time: 391 us; the launch traced here: 385 us
  waiting for transfers between devices  176 us (45%)
  local copies, waits for them, and re-layouts  87.6 us (22%)
  matrix products  57.8 us (15%)
  starting transfers between devices  25.5 us (7%)
  blocking collectives  18.8 us (5%)
  between operations  14 us (4%)
  other arithmetic  5.58 us (1%)
    all_gather x1, waiting for transfers between devices, shards(): lax.all_gather(out_weight, 'seq', axis=0, tiled=True)  143 us
    gather x3, local copies, waits for them, and re-layouts, shards(): picked = jnp.take(stream, source, axis=1).astype(jnp.float32)  62 us
    dot_general x12, matrix products, matmul_last(): return jnp.einsum('bkm,mj->bkj', left, right, precision=dft_precision)  39.4 us
    all_gather x1, waiting for transfers between devices, shards(): features = lax.all_gather(gated, 'chan', axis=1, tiled=True)  26.6 us
    all_to_all x1, blocking collectives, shards(): lax.all_to_all(gated_cols, 'seq', split_axis=1, concat_axis=0, tiled=True)  18.8 us
    gather x2, local copies, waits for them, and re-layouts, shards(): conv_sent = jnp.take(convolved, target, axis=1).astype(jnp.bfloat16)  14.1 us
    all_to_all x1, starting transfers between devices, shards(): lax.all_to_all(filter_taps, 'seq', split_axis=0, concat_axis=1, tiled=True)  12 us
    dot_general x1, matrix products, shards(): jnp.dot(features, lax.all_gather(out_weight, 'seq', axis=0, tiled=True),...  9.47 us
  transfers between devices with their start and end apart: 5, of which 4 were waited for; matrix products, arithmetic and copies ran while one was open for 36% of the time, Pallas kernels for 0%

commit v1 on v0

v1 whole, which is shorter than its diff:
```python
import functools

import jax
import jax.numpy as jnp
import ml_dtypes
import numpy as np
from jax import lax
from jax.experimental import pallas as pl
from jax.experimental.pallas import tpu as pltpu
from jax.sharding import PartitionSpec as P

NX, NY, NZ = 4, 4, 8
NS = NY * NZ
BLK = 128
CH = 32
REC = 8
DB = 17
ROWS = 40
MESH = pl.DeviceIdType.MESH
bf16 = jnp.bfloat16
f32 = jnp.float32


def coords():
    s = lax.axis_index("seq")
    c = lax.axis_index("chan")
    return c // 2, c % 2, s // NZ, s % NZ


def dev(x, core, y, z):
    return (y * NZ + z, x * 2 + core)


def signal(sem, device):
    pl.semaphore_signal(sem, inc=1, device_id=device, device_id_type=MESH)


def remote(src, dst, send, recv, device):
    return pltpu.make_async_remote_copy(
        src_ref=src, dst_ref=dst, send_sem=send, recv_sem=recv, device_id=device, device_id_type=MESH
    )


class Ring:
    def __init__(self, wt, send, recv, x, core, y, z):
        self.wt, self.send, self.recv, self.y = wt, send, recv, y
        self.up = dev(x, core, (y + 1) % NY, z)
        self.down = dev(x, core, (y + NY - 1) % NY, z)
        self.half = wt.shape[1] // 2

    def copy(self, slot, part, k, device):
        ref = self.wt.at[slot, pl.ds(part * self.half, self.half)]
        return remote(ref, ref, self.send.at[k], self.recv.at[k], device)

    def first(self):
        y = self.y
        return [
            self.copy(y, 0, 0, self.up),
            self.copy(y, 1, 1, self.down),
            self.copy(y, 1, 2, self.up),
            self.copy(y, 0, 3, self.down),
        ]

    def forward(self):
        y = self.y
        return [
            self.copy((y + NY - 1) % NY, 0, 4, self.up),
            self.copy((y + 1) % NY, 1, 5, self.down),
        ]

    def start(self):
        for c in self.first():
            c.start()

    def pass_on(self):
        first, forward = self.first(), self.forward()
        for k in range(2):
            first[k].wait_recv()
            forward[k].start()

    def finish_recv(self):
        for c in self.first()[2:] + self.forward():
            c.wait_recv()

    def finish_send(self):
        for c in self.first() + self.forward():
            c.wait_send()


def exchange_kernel(q_ref, k_ref, v_ref, t_ref, w_ref, rx, wt, w2, tx, ssem, rsem, wsend, wrecv):
    x, core, y, z = coords()
    barrier = pltpu.get_barrier_semaphore()
    up, down = dev(x, core, (y + 1) % NY, z), dev(x, core, (y + NY - 1) % NY, z)
    signal(barrier, up)
    signal(barrier, down)

    @pl.loop(0, NS)
    def _(i):
        @pl.when(jnp.logical_not((z // 4 == core) & (i == y * NZ + z)))
        def _():
            signal(barrier, (i, x * 2 + z // 4))

    for c in range(8):
        cols = pl.ds(c * BLK, BLK)
        prod = (k_ref[:, cols].astype(f32) * v_ref[:, cols].astype(f32)).T
        tx[pl.ds(4 * c, 4), pl.ds(0, CH), :] = prod.astype(bf16).reshape(4, CH, BLK)
        gate = q_ref[:, cols].astype(f32).T
        tx[pl.ds(4 * c, 4), pl.ds(48, CH), :] = gate.astype(bf16).reshape(4, CH, BLK)
    taps = t_ref[...].reshape(NS, CH, 64)
    taps = jnp.concatenate([taps[:, :16], taps[:, 16:]], axis=2)
    tx[:, pl.ds(CH, 16), :] = taps.astype(bf16)

    own = (z // 4 == core).astype(jnp.int32)
    pl.semaphore_wait(barrier, NS - own + 2)

    def piece(i):
        p = (i + 8 * (z % 4) + 4 * core + y) % NS
        to = dev(x, (p // 4) % 2, p % 4, 4 * core + p // 8)
        here = (own == 1) & (i == 0)
        far = remote(tx.at[p], rx.at[y * NZ + z], ssem.at[i], rsem, to)
        near = pltpu.make_async_copy(tx.at[p], rx.at[y * NZ + z], rsem)
        return here, far, near

    @pl.loop(0, NS)
    def _(i):
        here, far, near = piece(i)
        pl.when(here)(near.start)
        pl.when(jnp.logical_not(here))(far.start)

    for c in range(4):
        wt[y, pl.ds(c * BLK, BLK), :] = w_ref[:, pl.ds(c * BLK, BLK)].astype(f32).T.astype(bf16)
    ring = Ring(wt, wsend, wrecv, x, core, y, z)
    ring.start()
    for c in range(4):
        w2[pl.ds(c * BLK, BLK), :] = w_ref[:, pl.ds(512 + c * BLK, BLK)].astype(f32).T.astype(bf16)
    ring.pass_on()

    @pl.loop(0, NS)
    def _(i):
        here, far, _ = piece(i)
        pl.when(jnp.logical_not(here))(far.wait_send)

    pltpu.make_async_copy(tx, rx, rsem).wait()
    ring.finish_recv()
    ring.finish_send()


def conv_kernel(len_ref, rx, fhi, flo, ihi, ilo, out, hcat, xrow, xh, gh, yh, yrow):
    lane16 = lax.broadcasted_iota(jnp.int32, (16, BLK), 1)
    lane = lax.broadcasted_iota(jnp.int32, (CH, BLK), 1)
    zero = jnp.zeros((CH, BLK), bf16)
    hcat[0, :, pl.ds(BLK, BLK)] = zero
    hcat[DB - 1, :, pl.ds(0, BLK)] = zero
    for d in range(DB - 1):
        a = rx[2 * d, pl.ds(CH, 16), :].astype(f32)
        b = rx[2 * d + 1, pl.ds(CH, 16), :].astype(f32)
        top = jnp.where(lane16 < 64, a, pltpu.roll(b, 64, 1))
        bottom = jnp.where(lane16 < 64, pltpu.roll(a, 64, 1), b)
        h = jnp.concatenate([top, bottom], axis=0).astype(bf16)
        hcat[d, :, pl.ds(0, BLK)] = h
        hcat[d + 1, :, pl.ds(BLK, BLK)] = h

    def dot(a, b):
        return jnp.dot(a, b, preferred_element_type=f32)

    taps = hcat[...].reshape(DB * CH, 2 * BLK)
    gh[...] = (dot(taps, fhi[...]) + dot(taps, flo[...])).reshape(DB, CH, 2 * BLK)

    records = []
    begin = jnp.int32(0)
    base = jnp.int32(0)
    for r in range(REC):
        end = begin + len_ref[r]
        b0 = begin // BLK
        count = (end - 1) // BLK - b0 + 1
        records.append((begin, end, b0, count, base))
        begin = end
        base = base + count

    def mask(begin, end, n):
        token = lane + n * BLK
        return (token >= begin) & (token < end)

    for begin, end, b0, count, first in records:

        @pl.loop(0, count)
        def _(i):
            row = rx[b0 + i, pl.ds(0, CH), :].astype(f32)
            xrow[first + i] = jnp.where(mask(begin, end, b0 + i), row, 0.0).astype(bf16)

    groups = (base + 7) // 8

    @pl.loop(0, groups)
    def _(g):
        rows = xrow[pl.ds(8 * g, 8)].reshape(8 * CH, BLK)
        spectrum = dot(rows, fhi[pl.ds(0, BLK), :]) + dot(rows, flo[pl.ds(0, BLK), :])
        xh[pl.ds(8 * g, 8)] = spectrum.reshape(8, CH, 2 * BLK)

    re, im = pl.ds(0, BLK), pl.ds(BLK, BLK)
    for _, _, _, count, first in records:

        @pl.loop(0, count)
        def _(i):
            def step(d, acc):
                acc_re, acc_im = acc
                xr, xi = xh[first + i - d, :, re], xh[first + i - d, :, im]
                gr, gi = gh[d, :, re], gh[d, :, im]
                return acc_re + (xr * gr - xi * gi), acc_im + (xr * gi + xi * gr)

            none = jnp.zeros((CH, BLK), f32)
            acc_re, acc_im = lax.fori_loop(0, i + 1, step, (none, none))
            yh[first + i, :, re] = acc_re
            yh[first + i, :, im] = acc_im

    @pl.loop(0, groups)
    def _(g):
        rows = yh[pl.ds(8 * g, 8)].reshape(8 * CH, 2 * BLK)
        hi = rows.astype(bf16)
        lo = (rows - hi.astype(f32)).astype(bf16)
        back = dot(hi, ihi[...]) + dot(lo, ihi[...]) + dot(hi, ilo[...])
        yrow[pl.ds(8 * g, 8)] = back.reshape(8, CH, BLK)

    for begin, end, b0, count, first in records:

        @pl.loop(0, count)
        def _(i):
            n = b0 + i
            gated = rx[n, pl.ds(48, CH), :].astype(f32) * yrow[first + i]
            out[n] = jnp.where(mask(begin, end, n), gated, out[n].astype(f32)).astype(bf16)


def project_kernel(
    g_ref, wa, w2, out, wb, gall, rbuf, sbuf, asend, arecv, bsend, brecv, csend, crecv, wsend, wrecv, zsend, zrecv
):
    x, core, y, z = coords()
    mate = dev(x, 1 - core, y, z)
    ys = [dev(x, core, (y + i) % NY, z) for i in range(1, NY)]
    xs = [dev((x + i) % NX, core, y, z) for i in range(1, NX)]
    zs = [dev(x, core, y, (z + 1) % NZ), dev(x, core, y, (z + NZ - 1) % NZ)]
    barrier = pltpu.get_barrier_semaphore()
    for d in ys + xs + zs + [mate]:
        signal(barrier, d)
    copy_w = pltpu.make_async_copy(w2, wb.at[y], wsend.at[6])
    copy_w.start()
    order = [[4], [3, 5], [2, 6], [1, 7], [0]]

    def block(rel):
        return (z + rel) % NZ

    def a_copies(rel):
        b = block(rel)
        dst = gall.at[b, x, core, pl.ds(CH * y, CH)]
        near = pltpu.make_async_copy(g_ref.at[y * NZ + b], dst, arecv.at[rel])
        far = [
            remote(g_ref.at[((y + i) % NY) * NZ + b], dst, asend.at[rel, i], arecv.at[rel], ys[i - 1])
            for i in range(1, NY)
        ]
        return near, far

    def b_copies(rel):
        ref = gall.at[block(rel), x, core]
        return [remote(ref, ref, bsend.at[rel, i], brecv.at[rel, i], xs[i - 1]) for i in range(1, NX)]

    def c_copy(rel):
        ref = gall.at[block(rel), :, core]
        return remote(ref, ref, csend.at[rel], crecv.at[rel], mate)

    pl.semaphore_wait(barrier, 9)
    for group in order:
        for rel in group:
            near, far = a_copies(rel)
            near.start()
            for c in far:
                c.start()
    copy_w.wait()
    ring = Ring(wb, wsend, wrecv, x, core, y, z)
    ring.start()
    for group in order:
        for rel in group:
            ref = gall.at[block(rel), x, core]
            pltpu.make_async_copy(ref, ref, arecv.at[rel]).wait()
            for c in b_copies(rel):
                c.start()

    def gather(step):
        for rel in order[step]:
            for c in b_copies(rel):
                c.wait_recv()
            c_copy(rel).start()
        for rel in order[step]:
            c_copy(rel).wait_recv()

    def z_copy(way, h, step):
        return remote(
            sbuf.at[way, h, step], rbuf.at[way, h, step], zsend.at[way, h, step], zrecv.at[way, h, step], zs[way]
        )

    def sends(way, h, step):
        return step < 4 and (step > 0 or way == h)

    def compute(h, step):
        w = wa if h == 0 else wb
        blocks = [block(rel) for rel in order[step]]
        ways = [h] if step == 0 else [0, 1]
        for way in ways:
            if step > 0 and sends(way, h, step - 1):
                z_copy(way, h, step - 1).wait_recv()
        for r in range(2):
            rows = pl.ds(256 * r, 256)
            acc = None
            for i in range(NX):
                sides = [gall[b, i].reshape(2 * BLK, BLK) for b in blocks]
                right = jnp.concatenate(sides, axis=1) if len(sides) > 1 else sides[0]
                term = jnp.dot(w[i, rows, :], right, preferred_element_type=f32)
                acc = term if acc is None else acc + term
            if step == 4:
                total = acc + rbuf[0, h, 3, rows, :].astype(f32) + rbuf[1, h, 3, rows, :].astype(f32)
                out[:, pl.ds(512 * h + 256 * r, 256)] = total.T.astype(bf16)
                continue
            for k, way in enumerate(ways):
                part = acc[:, k * BLK : (k + 1) * BLK]
                if step > 0 and sends(way, h, step - 1):
                    part = part + rbuf[way, h, step - 1, rows, :].astype(f32)
                sbuf[way, h, step, rows, :] = part.astype(bf16)
        if step < 4:
            for way in ways:
                z_copy(way, h, step).start()

    gather(0)
    compute(0, 0)
    ring.pass_on()
    gather(1)
    compute(0, 1)
    ring.finish_recv()
    compute(1, 0)
    gather(2)
    compute(0, 2)
    compute(1, 1)
    gather(3)
    compute(0, 3)
    compute(1, 2)
    gather(4)
    compute(0, 4)
    compute(1, 3)
    compute(1, 4)

    for rel in range(NZ):
        for c in a_copies(rel)[1] + b_copies(rel) + [c_copy(rel)]:
            c.wait_send()
    for way in range(2):
        for h in range(2):
            for step in range(4):
                if sends(way, h, step):
                    z_copy(way, h, step).wait_send()
    ring.finish_send()


def split(a):
    hi = a.astype(ml_dtypes.bfloat16)
    return hi, (a - hi.astype(np.float64)).astype(ml_dtypes.bfloat16)


def dft_tables():
    theta = 2.0 * np.pi * (np.arange(BLK) + 0.5) / (2 * BLK)
    angle = np.arange(2 * BLK)[:, None] * theta[None, :]
    sign = np.where(np.arange(2 * BLK) < BLK, 1.0, -1.0)[:, None]
    forward = sign * np.concatenate([np.cos(angle), -np.sin(angle)], axis=1)
    angle = theta[:, None] * np.arange(BLK)[None, :]
    inverse = np.concatenate([np.cos(angle), -np.sin(angle)], axis=0) / BLK
    return (*split(forward), *split(inverse))


VM = pl.BlockSpec(memory_space=pltpu.VMEM)
SM = pl.BlockSpec(memory_space=pltpu.SMEM)
shape = jax.ShapeDtypeStruct
DMA = pltpu.SemaphoreType.DMA


def conv_call(lengths, rx):
    return pl.pallas_call(
        conv_kernel,
        out_shape=shape((NS, CH, BLK), bf16),
        in_specs=[SM] + [VM] * 5,
        out_specs=VM,
        scratch_shapes=[
            pltpu.VMEM((DB, CH, 2 * BLK), bf16),
            pltpu.VMEM((ROWS, CH, BLK), bf16),
            pltpu.VMEM((ROWS, CH, 2 * BLK), f32),
            pltpu.VMEM((DB, CH, 2 * BLK), f32),
            pltpu.VMEM((ROWS, CH, 2 * BLK), f32),
            pltpu.VMEM((ROWS, CH, BLK), f32),
        ],
        compiler_params=pltpu.CompilerParams(vmem_limit_bytes=40 << 20),
        name="conv",
    )(lengths, rx, *[jnp.asarray(t) for t in dft_tables()])


def shards(q, k, v, taps, weight, lengths):
    rx, wa, w2 = pl.pallas_call(
        exchange_kernel,
        out_shape=(shape((NS, 80, BLK), bf16), shape((NY, 512, 256), bf16), shape((512, 256), bf16)),
        in_specs=[VM] * 5,
        out_specs=(VM, VM, VM),
        scratch_shapes=[
            pltpu.VMEM((NS, 80, BLK), bf16),
            DMA((NS,)),
            DMA,
            DMA((6,)),
            DMA((6,)),
        ],
        compiler_params=pltpu.CompilerParams(collective_id=0, has_side_effects=True, vmem_limit_bytes=40 << 20),
        name="exchange",
    )(q, k, v, taps, weight)
    gated = conv_call(lengths, rx)
    return pl.pallas_call(
        project_kernel,
        out_shape=shape((BLK, 1024), bf16),
        in_specs=[VM] * 3,
        out_specs=VM,
        scratch_shapes=[
            pltpu.VMEM((NY, 512, 256), bf16),
            pltpu.VMEM((NZ, NX, 2, BLK, BLK), bf16),
            pltpu.VMEM((2, 2, 4, 512, BLK), bf16),
            pltpu.VMEM((2, 2, 4, 512, BLK), bf16),
            DMA((NZ, 4)),
            DMA((NZ,)),
            DMA((NZ, 4)),
            DMA((NZ, 4)),
            DMA((NZ,)),
            DMA((NZ,)),
            DMA((7,)),
            DMA((6,)),
            DMA((2, 2, 4)),
            DMA((2, 2, 4)),
        ],
        compiler_params=pltpu.CompilerParams(collective_id=1, has_side_effects=True, vmem_limit_bytes=40 << 20),
        name="project",
    )(gated, wa, w2)


def solution(mesh):
    two = P("seq", "chan")
    in_specs = (two, two, two, P("chan", "seq"), two, P())
    return jax.shard_map(shards, mesh=mesh, in_specs=in_specs, out_specs=two, check_vma=False)
```

time: 391 us -> 82.7 us (0.21); the launches traced: 385 us -> 81.7 us
  waiting for transfers between devices: 176 us -> 0 us
  local copies, waits for them, and re-layouts: 87.6 us -> 4.45 us
  Pallas kernels: 0 us -> 77.2 us
  matrix products: 57.8 us -> 0 us
  starting transfers between devices: 25.5 us -> 0 us
  blocking collectives: 18.8 us -> 0 us
  between operations: 14 us -> 0.1 us
  other arithmetic: 5.58 us -> 0 us
    all_gather x2 -> x0, waiting for transfers between devices: 169 us -> none  [the longest x1 143 us: shards(): lax.all_gather(out_weight, 'seq', axis=0, tiled=True)]
    pallas_call x0 -> x3, Pallas kernels: none -> 77.2 us  [the longest x1 43.6 us: shards(): pl.pallas_call(project_kernel, out_shape=shape((BLK, 1024), bf16), in_spe...]
    gather x5 -> x0, local copies, waits for them, and re-layouts: 76.1 us -> none  [the longest x3 62 us: shards(): picked = jnp.take(stream, source, axis=1).astype(jnp.float32)]
    dot_general x19 -> x0, matrix products: 57.8 us -> none  [the longest x12 39.4 us: matmul_last(): return jnp.einsum('bkm,mj->bkj', left, right, precision=dft_precision)]
    all_to_all x3 -> x0, starting transfers between devices: 25.2 us -> none  [the longest x1 12 us: shards(): lax.all_to_all(filter_taps, 'seq', split_axis=0, concat_axis=1, tiled=True)]
    all_to_all x1 -> x0, blocking collectives: 18.8 us -> none  [shards(): lax.all_to_all(gated_cols, 'seq', split_axis=1, concat_axis=0, tiled=True)]
    all_to_all x3 -> x0, waiting for transfers between devices: 5.73 us -> none  [the longest x1 3.41 us: shards(): lax.all_to_all(product.T, 'seq', split_axis=0, concat_axis=1, tiled=True)]
  transfers between devices with their start and end apart: 5 -> 0, of which waited for: 4 -> 0; matrix products, arithmetic and copies ran while one was open for 36% -> 0% of each run, Pallas kernels for 0% -> 0%
where the time goes in v1:
time: 82.7 us; the launch traced here: 81.7 us
  Pallas kernels  77.2 us (93%)
  local copies, waits for them, and re-layouts  4.45 us (5%)
    pallas_call x1, Pallas kernels, shards(): pl.pallas_call(project_kernel, out_shape=shape((BLK, 1024), bf16), in_spe...  43.6 us
    pallas_call x1, Pallas kernels, shards(): pl.pallas_call(exchange_kernel, out_shape=(shape((NS, 80, BLK), bf16), sh...  27.5 us
    pallas_call x1, Pallas kernels, conv_call(): pl.pallas_call(conv_kernel, out_shape=shape((NS, CH, BLK), bf16), in_spec...  6.04 us
    unnamed x20, local copies, waits for them, and re-layouts  4.45 us

profile of v1, /device:TPU:1, one launch (start us, length us, event | category | flops | bytes accessed | tf_op | source)
XLA Modules:
  0.0 81.7 jit_solution(10710332713436170883)
XLA Ops:
  0.0 0.0 copy-start
  0.0 0.0 copy-start.1
  0.0 1.2 %copy.11.t_ref = f32[1024,64]{1,0:T(8,128)S(1)} copy(f32[1024,64]{0,1:T(8,128)} %param.13) | data formatting | bytes 524288 | tf_op args[3]
  1.2 0.0 copy-done
  1.2 0.0 copy-done.1
  1.2 0.0 copy-start.2
  1.3 0.9 %copy-done.2 = bf16[128,1024]{1,0:T(8,128)(2,1)S(1)} copy-done((bf16[128,1024]{1,0:T(8,128)(2,1)S(1)}, bf16[128,1024]{1,0:T(8,128)(2,1)}, u32[]{:S(2)}) %copy-start.2) | copy-done | bytes 262168
  2.2 0.0 copy-start.3
  2.2 0.9 %copy-done.3 = bf16[128,1024]{1,0:T(8,128)(2,1)S(1)} copy-done((bf16[128,1024]{1,0:T(8,128)(2,1)S(1)}, bf16[128,1024]{1,0:T(8,128)(2,1)}, u32[]{:S(2)}) %copy-start.3) | copy-done | bytes 262168
  3.2 0.0 copy-start.4
  3.2 0.0 copy-start.5
  3.2 0.0 copy-start.6
  3.2 0.0 copy-start.7
  3.2 27.5 %exchange.1 = (bf16[32,80,128]{2,1,0:T(8,128)(2,1)S(1)}, bf16[4,512,256]{2,1,0:T(8,128)(2,1)S(1)}, bf16[512,256]{1,0:T(8,128)(2,1)S(1)}) custom-call(bf16[128,1024]{1,0:T(8,128)(2,1)S(1)} %copy-done.1, bf16[128,1024]{1,0:T(8,128)(2,1)S(1)} %copy-done.2, bf16[128,1024]{1,0:T(8,128)(2,1)S(1)} %copy-done.3, f32[1024,64]{1,0:T(8,128)S(1)} %copy.11.t_ref, ...), custom_call_target="tpu_custom_call" | custom-call | tf_op jit(solution)/shard_map/exchange/pallas_call | solution.py:399
  30.7 0.0 copy-start.8
  30.7 0.0 copy-done.4
  30.7 0.0 copy-done.5
  30.7 0.0 copy-done.6
  30.7 0.0 copy-done.7
  30.7 0.6 copy-done.8
  31.4 6.0 %conv.1.g_ref = bf16[32,32,128]{2,1,0:T(8,128)(2,1)S(1)} custom-call(s32[8]{0:T(128)S(1)} %copy-done.8, bf16[32,80,128]{2,1,0:T(8,128)(2,1)S(1)} %get-tuple-element.8.rx, bf16[256,256]{1,0:T(8,128)(2,1)S(1)} %copy-done.5, bf16[256,256]{1,0:T(8,128)(2,1)S(1)} %copy-done.4, bf16[256,128]{1,0:T(8,128)(2,1)S(1)} %copy-done.7, bf16[256,128]{1,0:T(8,128)(2,1)S(1)} %copy-done.6), custom_call_target="tpu_custom_call" | custom-call | tf_op jit(solution)/shard_map/conv/pallas_call | solution.py:380
  37.4 43.6 %project.1 = bf16[128,1024]{1,0:T(8,128)(2,1)S(1)} custom-call(bf16[32,32,128]{2,1,0:T(8,128)(2,1)S(1)} %conv.1.g_ref, bf16[4,512,256]{2,1,0:T(8,128)(2,1)S(1)} %get-tuple-element.9.wa, bf16[512,256]{1,0:T(8,128)(2,1)S(1)} %get-tuple-element.10.w2), custom_call_target="tpu_custom_call" | custom-call | tf_op jit(solution)/shard_map/project/pallas_call | solution.py:415
  81.0 0.7 copy.13
Async XLA Ops:
  0.0 1.2 %copy-start = (bf16[256,1024]{1,0:T(8,128)(2,1)S(1)}, bf16[256,1024]{1,0:T(8,128)(2,1)}, u32[]{:S(2)}) copy-start(bf16[256,1024]{1,0:T(8,128)(2,1)} %w_ref.1) | copy-start | bytes 1572868
  0.0 1.2 %copy-start.1 = (bf16[128,1024]{1,0:T(8,128)(2,1)S(1)}, bf16[128,1024]{1,0:T(8,128)(2,1)}, u32[]{:S(2)}) copy-start(bf16[128,1024]{1,0:T(8,128)(2,1)} %q_ref.1) | copy-start | bytes 786436
  1.2 1.0 %copy-start.2 = (bf16[128,1024]{1,0:T(8,128)(2,1)S(1)}, bf16[128,1024]{1,0:T(8,128)(2,1)}, u32[]{:S(2)}) copy-start(bf16[128,1024]{1,0:T(8,128)(2,1)} %k_ref.1) | copy-start | bytes 786436
  2.2 0.9 %copy-start.3 = (bf16[128,1024]{1,0:T(8,128)(2,1)S(1)}, bf16[128,1024]{1,0:T(8,128)(2,1)}, u32[]{:S(2)}) copy-start(bf16[128,1024]{1,0:T(8,128)(2,1)} %v_ref.1) | copy-start | bytes 786436
  3.2 27.6 %copy-start.4 = (bf16[256,256]{1,0:T(8,128)(2,1)S(1)}, bf16[256,256]{1,0:T(8,128)(2,1)}, u32[]{:S(2)}) copy-start(bf16[256,256]{1,0:T(8,128)(2,1)} %constant.9.clone.flo) | copy-start | bytes 393220
  3.2 27.6 %copy-start.5 = (bf16[256,256]{1,0:T(8,128)(2,1)S(1)}, bf16[256,256]{1,0:T(8,128)(2,1)}, u32[]{:S(2)}) copy-start(bf16[256,256]{1,0:T(8,128)(2,1)} %constant.8.clone.fhi) | copy-start | bytes 393220
  3.2 27.6 %copy-start.6 = (bf16[256,128]{1,0:T(8,128)(2,1)S(1)}, bf16[256,128]{1,0:T(8,128)(2,1)}, u32[]{:S(2)}) copy-start(bf16[256,128]{1,0:T(8,128)(2,1)} %constant.11.clone.ilo) | copy-start | bytes 196612
  3.2 27.6 %copy-start.7 = (bf16[256,128]{1,0:T(8,128)(2,1)S(1)}, bf16[256,128]{1,0:T(8,128)(2,1)}, u32[]{:S(2)}) copy-start(bf16[256,128]{1,0:T(8,128)(2,1)} %constant.10.clone.ihi) | copy-start | bytes 196612
  30.7 0.7 copy-start.8

commit v2 on v0

v2 whole, which is shorter than its diff:
```python
import jax
import jax.numpy as jnp
import numpy as np
from jax import lax
from jax.experimental import pallas as pl
from jax.experimental.pallas import tpu as pltpu
from jax.sharding import PartitionSpec as P

NX, NY, NZ = 4, 4, 8
NS = NY * NZ
BLK = 128
CH = 32
REC = 8
DB = 17
MSG = 48
MESH = pl.DeviceIdType.MESH
bf16 = jnp.bfloat16
f32 = jnp.float32
ORDER = [4, 3, 5, 2, 6, 1, 7, 0]
STEPS = [[4], [3, 5], [2, 6], [1, 7], [0]]


def coords():
    s = lax.axis_index("seq")
    c = lax.axis_index("chan")
    return c // 2, c % 2, s // NZ, s % NZ


def dev(x, core, y, z):
    return (y * NZ + z, x * 2 + core)


def signal(sem, device):
    pl.semaphore_signal(sem, inc=1, device_id=device, device_id_type=MESH)


def remote(src, dst, send, recv, device):
    return pltpu.make_async_remote_copy(
        src_ref=src, dst_ref=dst, send_sem=send, recv_sem=recv, device_id=device, device_id_type=MESH
    )


def dot(a, b):
    return jnp.dot(a, b, preferred_element_type=f32)


class Ring:
    def __init__(self, wt, base, send, recv, x, core, y, z):
        self.wt, self.base, self.send, self.recv, self.y = wt, base, send, recv, y
        self.up = dev(x, core, (y + 1) % NY, z)
        self.down = dev(x, core, (y + NY - 1) % NY, z)

    def copy(self, slot, part, k, device):
        ref = self.wt.at[slot, pl.ds(self.base + part * 256, 256)]
        return remote(ref, ref, self.send.at[k], self.recv.at[k], device)

    def first(self):
        y = self.y
        return [
            self.copy(y, 0, 0, self.up),
            self.copy(y, 1, 1, self.down),
            self.copy(y, 1, 2, self.up),
            self.copy(y, 0, 3, self.down),
        ]

    def forward(self):
        y = self.y
        return [
            self.copy((y + NY - 1) % NY, 0, 4, self.up),
            self.copy((y + 1) % NY, 1, 5, self.down),
        ]

    def start(self):
        for c in self.first():
            c.start()

    def pass_on(self):
        first, forward = self.first(), self.forward()
        for k in range(2):
            first[k].wait_recv()
            forward[k].start()

    def finish_recv(self):
        for c in self.first()[2:] + self.forward():
            c.wait_recv()

    def finish_send(self):
        for c in self.first() + self.forward():
            c.wait_send()


def hyena_kernel(
    len_ref, q_hbm, k_hbm, v_hbm, t_hbm, w_hbm, tab_hbm, out,
    q_ref, k_ref, v_ref, t_ref, w_ref, tab_ref, tab, tx, rx, qt, qall, hcat, xrow, xh, gh, yh, ye, cv, wt, gall, sbuf, rbuf, seg,
    isem, ssem, rsem, qsend, qrecv, nsem, asend, arecv, bsend, brecv, csend, crecv, w0send, w0recv, w1send, w1recv,
    zsend, zrecv,
):
    x, core, y, z = coords()
    loads = [
        pltpu.make_async_copy(src, dst, isem.at[i])
        for i, (src, dst) in enumerate(
            [(k_hbm, k_ref), (v_hbm, v_ref), (t_hbm, t_ref), (w_hbm, w_ref), (q_hbm, q_ref), (tab_hbm, tab_ref)]
        )
    ]
    for c in loads:
        c.start()

    own = (z // 4 == core).astype(jnp.int32)
    mate = dev(x, 1 - core, y, z)
    ys = [dev(x, core, (y + i) % NY, z) for i in range(1, NY)]
    xs = [dev((x + i) % NX, core, y, z) for i in range(1, NX)]
    zs = [dev(x, core, y, (z + 1) % NZ), dev(x, core, y, (z + NZ - 1) % NZ)]
    barrier = pltpu.get_barrier_semaphore()
    for d in ys + xs + zs + [mate]:
        signal(barrier, d)

    @pl.loop(0, NS)
    def _(i):
        @pl.when(jnp.logical_not((own == 1) & (i == y * NZ + z)))
        def _():
            signal(barrier, (i, x * 2 + z // 4))

    loads[0].wait()
    loads[1].wait()
    for c in range(8):
        cols = pl.ds(c * BLK, BLK)
        prod = (k_ref[:, cols].astype(f32) * v_ref[:, cols].astype(f32)).T
        tx[pl.ds(4 * c, 4), pl.ds(0, CH), :] = prod.astype(bf16).reshape(4, CH, BLK)
    loads[2].wait()
    for c in range(8):
        taps = t_ref[:, pl.ds(c * BLK, BLK)].T.reshape(4, CH, 64)
        taps = jnp.concatenate([taps[:, :16], taps[:, 16:]], axis=2)
        tx[pl.ds(4 * c, 4), pl.ds(CH, 16), :] = taps.astype(bf16)

    pl.semaphore_wait(barrier, NS - own + 9)

    def piece(i):
        p = (i + 8 * (z % 4) + 4 * core + y) % NS
        to = dev(x, (p // 4) % 2, p % 4, 4 * core + p // 8)
        here = (own == 1) & (i == 0)
        src, dst = tx.at[p], rx.at[y * NZ + z]
        return here, src, dst, to

    @pl.loop(0, NS)
    def _(i):
        here, src, dst, to = piece(i)

        @pl.when(here)
        def _():
            pltpu.make_async_copy(src, dst, rsem).start()

        @pl.when(jnp.logical_not(here))
        def _():
            remote(src, dst, ssem.at[i], rsem, to).start()

    loads[3].wait()
    for c in range(4):
        wt[y, pl.ds(c * BLK, BLK), :] = w_ref[:, pl.ds(c * BLK, BLK)].astype(f32).T.astype(bf16)
    rings = [Ring(wt, 0, w0send, w0recv, x, core, y, z), Ring(wt, 512, w1send, w1recv, x, core, y, z)]
    rings[0].start()

    loads[4].wait()
    for c in range(8):
        qt[c] = q_ref[:, pl.ds(c * BLK, BLK)].astype(f32).T.astype(bf16)

    def q_piece(i):
        p = (i + 2 * (z % 4) + core) % 8
        to = dev(x, p % 2, y, 4 * core + p // 2)
        here = (own == 1) & (i == 0)
        return here, qt.at[p], qall.at[z], to

    @pl.loop(0, 8)
    def _(i):
        here, src, dst, to = q_piece(i)

        @pl.when(here)
        def _():
            pltpu.make_async_copy(src, dst, qrecv).start()

        @pl.when(jnp.logical_not(here))
        def _():
            remote(src, dst, qsend.at[i], qrecv, to).start()

    for c in range(4):
        wt[y, pl.ds(512 + c * BLK, BLK), :] = w_ref[:, pl.ds(512 + c * BLK, BLK)].astype(f32).T.astype(bf16)

    bounds = []
    begin = jnp.int32(0)
    for r in range(REC):
        bounds.append((begin, begin + len_ref[r]))
        begin = begin + len_ref[r]

    @pl.loop(0, NS)
    def _(n):
        t = n * BLK
        first, last, extra = bounds[0][0], bounds[0][1], jnp.int32(NS)
        for r in range(1, REC):
            past = bounds[r][0] <= t
            first = jnp.where(past, bounds[r][0], first)
            last = jnp.where(past, bounds[r][1], last)
            extra = jnp.where(past, NS + r, extra)
        block = first // BLK
        seg[0, n] = block
        seg[1, n] = last
        seg[2, n] = jnp.where(first == block * BLK, block, extra)

    loads[5].wait()
    for i, cols in enumerate((pl.ds(0, 2 * BLK), pl.ds(2 * BLK, BLK))):
        table = tab_ref[:, cols]
        hi = table.astype(bf16)
        lo = (table - hi.astype(f32)).astype(bf16)
        if i == 0:
            tab[0], tab[1] = hi, lo
            tab[2] = jnp.concatenate([hi[:BLK], lo[:BLK]], axis=0)
        else:
            tab[3] = jnp.concatenate([hi, lo], axis=1)
    pltpu.make_async_copy(tx, rx, rsem).wait()

    lane16 = lax.broadcasted_iota(jnp.int32, (16, BLK), 1)
    lane = lax.broadcasted_iota(jnp.int32, (CH, BLK), 1)
    zero = jnp.zeros((CH, BLK), bf16)
    hcat[0, :, pl.ds(BLK, BLK)] = zero
    hcat[DB - 1, :, pl.ds(0, BLK)] = zero

    @pl.loop(0, DB - 1)
    def _(d):
        a = rx[2 * d, pl.ds(CH, 16), :].astype(f32)
        b = rx[2 * d + 1, pl.ds(CH, 16), :].astype(f32)
        top = jnp.where(lane16 < 64, a, pltpu.roll(b, 64, 1))
        bottom = jnp.where(lane16 < 64, pltpu.roll(a, 64, 1), b)
        h = jnp.concatenate([top, bottom], axis=0).astype(bf16)
        hcat[d, :, pl.ds(0, BLK)] = h
        hcat[d + 1, :, pl.ds(BLK, BLK)] = h

    for lo, size in ((0, 8), (8, 9)):
        taps = hcat[pl.ds(lo, size)].reshape(size * CH, 2 * BLK)
        gh[pl.ds(lo, size)] = (dot(taps, tab[0]) + dot(taps, tab[1])).reshape(size, CH, 2 * BLK)

    @pl.loop(0, NS)
    def _(n):
        row = rx[n, pl.ds(0, CH), :].astype(f32)
        xrow[n] = jnp.where(lane + n * BLK < seg[1, n], row, 0.0).astype(bf16)

    xrow[NS] = zero
    for r in range(1, REC):
        begin, end = bounds[r]
        n = begin // BLK
        token = lane + n * BLK
        row = rx[n, pl.ds(0, CH), :].astype(f32)
        xrow[NS + r] = jnp.where((token >= begin) & (token < end), row, 0.0).astype(bf16)

    @pl.loop(0, 5)
    def _(g):
        rows = xrow[pl.ds(8 * g, 8)].reshape(8 * CH, BLK)
        spectrum = dot(jnp.concatenate([rows, rows], axis=1), tab[2])
        xh[pl.ds(8 * g, 8)] = spectrum.reshape(8, CH, 2 * BLK)

    re, im = pl.ds(0, BLK), pl.ds(BLK, BLK)

    def inverse(rows):
        hi = rows.astype(bf16)
        lo = (rows - hi.astype(f32)).astype(bf16)
        both = dot(hi, tab[3])
        return both[:, :BLK] + both[:, BLK:] + dot(lo, tab[3, :, :BLK])

    gr, gi = gh[0, :, re], gh[0, :, im]
    for r in range(REC):
        xr, xi = xh[NS + r, :, re], xh[NS + r, :, im]
        ye[r, :, re] = xr * gr - xi * gi
        ye[r, :, im] = xr * gi + xi * gr
    ye[:, :, re] = inverse(ye[...].reshape(REC * CH, 2 * BLK)).reshape(REC, CH, BLK)

    rings[0].pass_on()

    def place(rel):
        return (z + rel) % NZ

    def convolve(rel):
        b = place(rel)

        @pl.loop(0, NY)
        def _(j):
            n = j * NZ + b
            block, first = seg[0, n], seg[2, n]
            acc_re = jnp.zeros((CH, BLK), f32)
            acc_im = jnp.zeros((CH, BLK), f32)
            for d in range(DB):
                m = n - d
                row = jnp.where(m > block, m, jnp.where(m == block, first, NS))
                xr, xi = xh[row, :, re], xh[row, :, im]
                gr, gi = gh[d, :, re], gh[d, :, im]
                acc_re = acc_re + (xr * gr - xi * gi)
                acc_im = acc_im + (xr * gi + xi * gr)
            yh[j, :, re] = acc_re
            yh[j, :, im] = acc_im

        back = inverse(yh[...].reshape(NY * CH, 2 * BLK)).reshape(NY, CH, BLK)
        for j in range(NY):
            n = j * NZ + b
            token = lane + n * BLK
            value = back[j]
            for r in range(1, REC):
                begin, end = bounds[r]
                low = jnp.where(begin > n * BLK, begin, TOKENS_END)
                value = jnp.where((token >= low) & (token < end), ye[r, :, re], value)
            cv[rel, j] = value.astype(bf16)

    def a_dst(rel):
        return gall.at[place(rel), x, core, pl.ds(CH * y, CH)]

    def a_near(rel):
        return pltpu.make_async_copy(cv.at[rel, y], a_dst(rel), arecv.at[rel])

    def a_far(rel):
        return [
            remote(cv.at[rel, (y + i) % NY], a_dst(rel), asend.at[rel, i], arecv.at[rel], ys[i - 1])
            for i in range(1, NY)
        ]

    def b_copies(rel):
        ref = gall.at[place(rel), x, core]
        return [remote(ref, ref, bsend.at[rel, i], brecv.at[rel, i], xs[i - 1]) for i in range(1, NX)]

    def c_copy(rel):
        ref = gall.at[place(rel), :, core]
        return remote(ref, ref, csend.at[rel], crecv.at[rel], mate)

    def conv(i):
        rel = ORDER[i]
        convolve(rel)
        for c in a_far(rel):
            c.start()
        a_near(rel).start()

    def spread(i):
        rel = ORDER[i]
        b = place(rel)
        ref = gall.at[b, x, core]
        pltpu.make_async_copy(ref, ref, arecv.at[rel]).wait()
        gall[b, x, core] = (gall[b, x, core].astype(f32) * qall[b].astype(f32)).astype(bf16)
        for c in b_copies(rel):
            c.start()

    def share(i):
        rel = ORDER[i]
        for c in b_copies(rel):
            c.wait_recv()
        c_copy(rel).start()

    def ready(i):
        c_copy(ORDER[i]).wait_recv()

    def z_copy(way, h, step):
        return remote(
            sbuf.at[way, h, step], rbuf.at[way, h, step], zsend.at[way, h, step], zrecv.at[way, h, step], zs[way]
        )

    def sends(way, h, step):
        return step < 4 and (step > 0 or way == h % 2)

    def unit(h, step):
        blocks = [place(rel) for rel in STEPS[step]]
        ways = [h % 2] if step == 0 else [0, 1]
        rows = pl.ds(256 * h, 256)
        acc = None
        for i in range(NX):
            sides = [gall[b, i].reshape(2 * BLK, BLK) for b in blocks]
            right = jnp.concatenate(sides, axis=1) if len(sides) > 1 else sides[0]
            term = dot(wt[i, rows, :], right)
            acc = term if acc is None else acc + term
        for way in ways:
            if step > 0 and sends(way, h, step - 1):
                z_copy(way, h, step - 1).wait_recv()
        if step == 4:
            total = acc + rbuf[0, h, 3].astype(f32) + rbuf[1, h, 3].astype(f32)
            out[:, pl.ds(256 * h, 256)] = total.T.astype(bf16)
            return
        for i, way in enumerate(ways):
            part = acc[:, i * BLK : (i + 1) * BLK]
            if step > 0 and sends(way, h, step - 1):
                part = part + rbuf[way, h, step - 1].astype(f32)
            sbuf[way, h, step] = part.astype(bf16)
            z_copy(way, h, step).start()

    conv(0)
    conv(1)
    conv(2)
    pltpu.make_async_copy(qt, qall, qrecv).wait()
    spread(0)
    conv(3)
    spread(1)
    conv(4)
    spread(2)
    conv(5)
    spread(3)
    conv(6)
    share(0)
    spread(4)
    conv(7)
    rings[1].start()
    rings[0].finish_recv()
    ready(0)
    unit(0, 0)
    unit(1, 0)
    spread(5)
    share(1)
    share(2)
    spread(6)
    spread(7)
    ready(1)
    ready(2)
    unit(0, 1)
    unit(1, 1)
    share(3)
    share(4)
    rings[1].pass_on()
    ready(3)
    ready(4)
    unit(0, 2)
    unit(1, 2)
    rings[1].finish_recv()
    unit(2, 0)
    unit(3, 0)
    share(5)
    share(6)
    unit(2, 1)
    unit(3, 1)
    ready(5)
    ready(6)
    unit(0, 3)
    unit(1, 3)
    share(7)
    unit(2, 2)
    unit(3, 2)
    ready(7)
    unit(2, 3)
    unit(3, 3)
    for h in range(4):
        unit(h, 4)

    @pl.loop(0, NS)
    def _(i):
        here, src, dst, to = piece(i)

        @pl.when(jnp.logical_not(here))
        def _():
            remote(src, dst, ssem.at[i], rsem, to).wait_send()

    @pl.loop(0, 8)
    def _(i):
        here, src, dst, to = q_piece(i)

        @pl.when(jnp.logical_not(here))
        def _():
            remote(src, dst, qsend.at[i], qrecv, to).wait_send()

    for rel in range(NZ):
        for c in a_far(rel) + b_copies(rel) + [c_copy(rel)]:
            c.wait_send()
    for way in range(2):
        for h in range(4):
            for step in range(4):
                if sends(way, h, step):
                    z_copy(way, h, step).wait_send()
    for ring in rings:
        ring.finish_send()


TOKENS_END = NS * BLK


def dft_tables():
    theta = 2.0 * np.pi * (np.arange(BLK) + 0.5) / (2 * BLK)
    angle = np.arange(2 * BLK)[:, None] * theta[None, :]
    sign = np.where(np.arange(2 * BLK) < BLK, 1.0, -1.0)[:, None]
    forward = sign * np.concatenate([np.cos(angle), -np.sin(angle)], axis=1)
    angle = theta[:, None] * np.arange(BLK)[None, :]
    inverse = np.concatenate([np.cos(angle), -np.sin(angle)], axis=0) / BLK
    return np.concatenate([forward, inverse], axis=1).astype(np.float32)


def shards(q, k, v, taps, weight, lengths):
    vm = pl.BlockSpec(memory_space=pltpu.VMEM)
    hbm = pl.BlockSpec(memory_space=pl.ANY)
    dma = pltpu.SemaphoreType.DMA
    scratch = [
        ((BLK, 1024), bf16),
        ((BLK, 1024), bf16),
        ((BLK, 1024), bf16),
        ((64, 1024), f32),
        ((256, 1024), bf16),
        ((256, 384), f32),
        ((4, 256, 256), bf16),
        ((NS, MSG, BLK), bf16),
        ((NS, MSG, BLK), bf16),
        ((8, BLK, BLK), bf16),
        ((8, BLK, BLK), bf16),
        ((DB, CH, 2 * BLK), bf16),
        ((NS + REC, CH, BLK), bf16),
        ((NS + REC, CH, 2 * BLK), f32),
        ((DB, CH, 2 * BLK), f32),
        ((NY, CH, 2 * BLK), f32),
        ((REC, CH, 2 * BLK), f32),
        ((NZ, NY, CH, BLK), bf16),
        ((NY, 1024, 256), bf16),
        ((NZ, NX, 2, BLK, BLK), bf16),
        ((2, 4, 4, 256, BLK), bf16),
        ((2, 4, 4, 256, BLK), bf16),
    ]
    semaphores = [
        dma((6,)), dma((NS,)), dma, dma((8,)), dma, dma, dma((NZ, NY)), dma((NZ,)), dma((NZ, NX)), dma((NZ, NX)),
        dma((NZ,)), dma((NZ,)), dma((6,)), dma((6,)), dma((6,)), dma((6,)), dma((2, 4, 4)), dma((2, 4, 4)),
    ]
    return pl.pallas_call(
        hyena_kernel,
        out_shape=jax.ShapeDtypeStruct((BLK, 1024), bf16),
        in_specs=[pl.BlockSpec(memory_space=pltpu.SMEM)] + [hbm] * 6,
        out_specs=vm,
        scratch_shapes=[pltpu.VMEM(*s) for s in scratch] + [pltpu.SMEM((3, NS), jnp.int32)] + semaphores,
        compiler_params=pltpu.CompilerParams(collective_id=0, has_side_effects=True, vmem_limit_bytes=60 << 20),
        name="hyena",
    )(lengths, q, k, v, taps.T, weight, jnp.asarray(dft_tables()))


def solution(mesh):
    two = P("seq", "chan")
    in_specs = (two, two, two, P("chan", "seq"), two, P())
    return jax.shard_map(shards, mesh=mesh, in_specs=in_specs, out_specs=two, check_vma=False)
```

time: 391 us -> 75.6 us (0.19)
  the two profiles are of different devices: /device:TPU:1 before, /device:TPU:8 now
where the time goes in v2:
time: 75.6 us; the launch traced here: 75.5 us
  Pallas kernels  73.8 us (98%)
  local copies, waits for them, and re-layouts  1.67 us (2%)
    pallas_call x1, Pallas kernels, shards(): pl.pallas_call(hyena_kernel, out_shape=jax.ShapeDtypeStruct((BLK, 1024),...  73.8 us
    unnamed x1, local copies, waits for them, and re-layouts  1.67 us

profile of v2, /device:TPU:8, one launch (start us, length us, event | category | flops | bytes accessed | tf_op | source)
XLA Modules:
  0.0 75.5 jit_solution(13518525104075974360)
XLA Ops:
  0.0 73.8 %hyena.1 = bf16[128,1024]{1,0:T(8,128)(2,1)} custom-call(s32[8]{0:T(128)} %len_ref.1, bf16[128,1024]{1,0:T(8,128)(2,1)} %q_hbm.1, bf16[128,1024]{1,0:T(8,128)(2,1)} %k_hbm.1, bf16[128,1024]{1,0:T(8,128)(2,1)} %v_hbm.1, f32[64,1024]{1,0:T(8,128)} %bitcast.1, bf16[256,1024]{1,0:T(8,128)(2,1)} %w_hbm.1, f32[256,384]{1,0:T(8,128)} %constant.2.clone.tab_hbm), custom_call_target="tpu_custom_call" | custom-call | tf_op jit(solution)/shard_map/hyena/pallas_call | solution.py:514
  73.8 1.7 %copy.9 = bf16[128,1024]{1,0:T(8,128)(2,1)} copy(bf16[128,1024]{1,0:T(8,128)(2,1)} %hyena.1) | data formatting | bytes 524288

commit v3 on v2

--- a/solution.py
+++ b/solution.py
@@ -12,12 +12,12 @@
 CH = 32
 REC = 8
 DB = 17
-MSG = 48
 MESH = pl.DeviceIdType.MESH
 bf16 = jnp.bfloat16
 f32 = jnp.float32
 ORDER = [4, 3, 5, 2, 6, 1, 7, 0]
-STEPS = [[4], [3, 5], [2, 6], [1, 7], [0]]
+FAR = [2, 1, 3]
+CHAINS = [(0, 0), (1, 1), (0, 1), (2, 0), (1, 2), (3, 1), (0, 2), (2, 1), (1, 3), (3, 2), (2, 2), (0, 3), (3, 3), (2, 3)]
 
 
 def coords():
@@ -51,7 +51,7 @@
         self.down = dev(x, core, (y + NY - 1) % NY, z)
 
     def copy(self, slot, part, k, device):
-        ref = self.wt.at[slot, pl.ds(self.base + part * 256, 256)]
+        ref = self.wt.at[pl.ds(self.base + part * 256, 256), pl.ds(pl.multiple_of(slot * 256, 256), 256)]
         return remote(ref, ref, self.send.at[k], self.recv.at[k], device)
 
     def first(self):
@@ -70,8 +70,8 @@
             self.copy((y + 1) % NY, 1, 5, self.down),
         ]
 
-    def start(self):
-        for c in self.first():
+    def start(self, part):
+        for c in self.first()[2 * part : 2 * part + 2]:
             c.start()
 
     def pass_on(self):
@@ -90,8 +90,8 @@
 
 
 def hyena_kernel(
-    len_ref, q_hbm, k_hbm, v_hbm, t_hbm, w_hbm, tab_hbm, out,
-    q_ref, k_ref, v_ref, t_ref, w_ref, tab_ref, tab, tx, rx, qt, qall, hcat, xrow, xh, gh, yh, ye, cv, wt, gall, sbuf, rbuf, seg,
+    len_hbm, q_hbm, k_hbm, v_hbm, t_hbm, w_hbm, tab_hbm, out,
+    q_ref, k_ref, v_ref, t_ref, w_ref, tab_ref, tab, tx, rx, qt, qall, hcat, xrow, xh, gh, yh, ye, cv, wt, gall, sbuf, rbuf, seg, len_ref,
     isem, ssem, rsem, qsend, qrecv, nsem, asend, arecv, bsend, brecv, csend, crecv, w0send, w0recv, w1send, w1recv,
     zsend, zrecv,
 ):
@@ -99,7 +99,7 @@
     loads = [
         pltpu.make_async_copy(src, dst, isem.at[i])
         for i, (src, dst) in enumerate(
-            [(k_hbm, k_ref), (v_hbm, v_ref), (t_hbm, t_ref), (w_hbm, w_ref), (q_hbm, q_ref), (tab_hbm, tab_ref)]
+            [(k_hbm, k_ref), (v_hbm, v_ref), (t_hbm, t_ref), (w_hbm, w_ref), (q_hbm, q_ref), (tab_hbm, tab_ref), (len_hbm, len_ref)]
         )
     ]
     for c in loads:
@@ -107,8 +107,8 @@
 
     own = (z // 4 == core).astype(jnp.int32)
     mate = dev(x, 1 - core, y, z)
-    ys = [dev(x, core, (y + i) % NY, z) for i in range(1, NY)]
-    xs = [dev((x + i) % NX, core, y, z) for i in range(1, NX)]
+    ys = [dev(x, core, (y + i) % NY, z) for i in FAR]
+    xs = [dev((x + i) % NX, core, y, z) for i in FAR]
     zs = [dev(x, core, y, (z + 1) % NZ), dev(x, core, y, (z + NZ - 1) % NZ)]
     barrier = pltpu.get_barrier_semaphore()
     for d in ys + xs + zs + [mate]:
@@ -120,12 +120,6 @@
         def _():
             signal(barrier, (i, x * 2 + z // 4))
 
-    loads[0].wait()
-    loads[1].wait()
-    for c in range(8):
-        cols = pl.ds(c * BLK, BLK)
-        prod = (k_ref[:, cols].astype(f32) * v_ref[:, cols].astype(f32)).T
-        tx[pl.ds(4 * c, 4), pl.ds(0, CH), :] = prod.astype(bf16).reshape(4, CH, BLK)
     loads[2].wait()
     for c in range(8):
         taps = t_ref[:, pl.ds(c * BLK, BLK)].T.reshape(4, CH, 64)
@@ -134,30 +128,53 @@
 
     pl.semaphore_wait(barrier, NS - own + 9)
 
+    def chunk(i):
+        return (i + 2 * (z % 4) + core) % 8
+
     def piece(i):
-        p = (i + 8 * (z % 4) + 4 * core + y) % NS
-        to = dev(x, (p // 4) % 2, p % 4, 4 * core + p // 8)
-        here = (own == 1) & (i == 0)
-        src, dst = tx.at[p], rx.at[y * NZ + z]
-        return here, src, dst, to
-
-    @pl.loop(0, NS)
+        c = chunk(i // 4)
+        yy = (y + (6 - i % 4) % 4) % NY
+        to = dev(x, c % 2, yy, 4 * core + c // 2)
+        here = (own == 1) & (c == 2 * (z % 4) + core) & (yy == y)
+        return here, 4 * c + yy, to
+
+    def post(i, src, dst, send, recv):
+        here, p, to = piece(i)
+
+        @pl.when(here)
+        def _():
+            pltpu.make_async_copy(src.at[p], dst.at[y * NZ + z], recv).start()
+
+        @pl.when(jnp.logical_not(here))
+        def _():
+            remote(src.at[p], dst.at[y * NZ + z], send.at[i], recv, to).start()
+
+    def posted(i, src, dst, send, recv):
+        here, p, to = piece(i)
+
+        @pl.when(jnp.logical_not(here))
+        def _():
+            remote(src.at[p], dst.at[y * NZ + z], send.at[i], recv, to).wait_send()
+
+    for c in loads[:2]:
+        c.wait()
+
+    @pl.loop(0, 8)
     def _(i):
-        here, src, dst, to = piece(i)
-
-        @pl.when(here)
-        def _():
-            pltpu.make_async_copy(src, dst, rsem).start()
-
-        @pl.when(jnp.logical_not(here))
-        def _():
-            remote(src, dst, ssem.at[i], rsem, to).start()
+        c = chunk(i)
+        cols = pl.ds(pl.multiple_of(c * BLK, BLK), BLK)
+        prod = (k_ref[:, cols].astype(f32) * v_ref[:, cols].astype(f32)).T
+        tx[pl.ds(4 * c, 4), pl.ds(0, CH), :] = prod.astype(bf16).reshape(4, CH, BLK)
+        for j in range(NY):
+            post(4 * i + j, tx, rx, ssem, rsem)
 
     loads[3].wait()
+    w_cols = pl.ds(pl.multiple_of(y * 256, 256), 256)
     for c in range(4):
-        wt[y, pl.ds(c * BLK, BLK), :] = w_ref[:, pl.ds(c * BLK, BLK)].astype(f32).T.astype(bf16)
+        wt[pl.ds(c * BLK, BLK), w_cols] = w_ref[:, pl.ds(c * BLK, BLK)].astype(f32).T.astype(bf16)
     rings = [Ring(wt, 0, w0send, w0recv, x, core, y, z), Ring(wt, 512, w1send, w1recv, x, core, y, z)]
-    rings[0].start()
+    rings[0].start(0)
+    rings[0].start(1)
 
     loads[4].wait()
     for c in range(8):
@@ -182,8 +199,9 @@
             remote(src, dst, qsend.at[i], qrecv, to).start()
 
     for c in range(4):
-        wt[y, pl.ds(512 + c * BLK, BLK), :] = w_ref[:, pl.ds(512 + c * BLK, BLK)].astype(f32).T.astype(bf16)
-
+        wt[pl.ds(512 + c * BLK, BLK), w_cols] = w_ref[:, pl.ds(512 + c * BLK, BLK)].astype(f32).T.astype(bf16)
+
+    loads[6].wait()
     bounds = []
     begin = jnp.int32(0)
     for r in range(REC):
@@ -214,6 +232,8 @@
             tab[2] = jnp.concatenate([hi[:BLK], lo[:BLK]], axis=0)
         else:
             tab[3] = jnp.concatenate([hi, lo], axis=1)
+    rings[0].pass_on()
+    rings[1].start(0)
     pltpu.make_async_copy(tx, rx, rsem).wait()
 
     lane16 = lax.broadcasted_iota(jnp.int32, (16, BLK), 1)
@@ -269,8 +289,6 @@
         ye[r, :, re] = xr * gr - xi * gi
         ye[r, :, im] = xr * gi + xi * gr
     ye[:, :, re] = inverse(ye[...].reshape(REC * CH, 2 * BLK)).reshape(REC, CH, BLK)
-
-    rings[0].pass_on()
 
     def place(rel):
         return (z + rel) % NZ
@@ -313,13 +331,13 @@
 
     def a_far(rel):
         return [
-            remote(cv.at[rel, (y + i) % NY], a_dst(rel), asend.at[rel, i], arecv.at[rel], ys[i - 1])
-            for i in range(1, NY)
+            remote(cv.at[rel, (y + i) % NY], a_dst(rel), asend.at[rel, i], arecv.at[rel], d)
+            for i, d in zip(FAR, ys)
         ]
 
     def b_copies(rel):
         ref = gall.at[place(rel), x, core]
-        return [remote(ref, ref, bsend.at[rel, i], brecv.at[rel, i], xs[i - 1]) for i in range(1, NX)]
+        return [remote(ref, ref, bsend.at[rel, i], brecv.at[rel, i], d) for i, d in enumerate(xs)]
 
     def c_copy(rel):
         ref = gall.at[place(rel), :, core]
@@ -358,93 +376,59 @@
     def sends(way, h, step):
         return step < 4 and (step > 0 or way == h % 2)
 
-    def unit(h, step):
-        blocks = [place(rel) for rel in STEPS[step]]
-        ways = [h % 2] if step == 0 else [0, 1]
-        rows = pl.ds(256 * h, 256)
-        acc = None
-        for i in range(NX):
-            sides = [gall[b, i].reshape(2 * BLK, BLK) for b in blocks]
-            right = jnp.concatenate(sides, axis=1) if len(sides) > 1 else sides[0]
-            term = dot(wt[i, rows, :], right)
-            acc = term if acc is None else acc + term
-        for way in ways:
-            if step > 0 and sends(way, h, step - 1):
-                z_copy(way, h, step - 1).wait_recv()
-        if step == 4:
-            total = acc + rbuf[0, h, 3].astype(f32) + rbuf[1, h, 3].astype(f32)
-            out[:, pl.ds(256 * h, 256)] = total.T.astype(bf16)
-            return
-        for i, way in enumerate(ways):
-            part = acc[:, i * BLK : (i + 1) * BLK]
-            if step > 0 and sends(way, h, step - 1):
-                part = part + rbuf[way, h, step - 1].astype(f32)
-            sbuf[way, h, step] = part.astype(bf16)
-            z_copy(way, h, step).start()
-
-    conv(0)
-    conv(1)
-    conv(2)
+    def rows(h):
+        return pl.ds(256 * h, 256)
+
+    def term(h, rel):
+        return dot(wt[rows(h), :], gall[place(rel)].reshape(1024, BLK))
+
+    def ring_send(h, step):
+        for way in range(2):
+            k = h ^ way
+            total = term(k, 4 - step if way == 0 else 4 + step)
+            if step > 0 and sends(way, k, step - 1):
+                z_copy(way, k, step - 1).wait_recv()
+                total = total + rbuf[way, k, step - 1].astype(f32)
+            sbuf[way, k, step] = total.astype(bf16)
+            z_copy(way, k, step).start()
+
+    def ring_end():
+        terms = [term(h, 0) for h in range(4)]
+        for h in (0, 1, 2, 3):
+            total = terms[h]
+            for way in range(2):
+                z_copy(way, h, 3).wait_recv()
+                total = total + rbuf[way, h, 3].astype(f32)
+            out[:, rows(h)] = total.T.astype(bf16)
+
+    for i in range(5):
+        conv(i)
     pltpu.make_async_copy(qt, qall, qrecv).wait()
-    spread(0)
-    conv(3)
-    spread(1)
-    conv(4)
-    spread(2)
-    conv(5)
-    spread(3)
-    conv(6)
-    share(0)
-    spread(4)
-    conv(7)
-    rings[1].start()
+    for i in range(3):
+        spread(i)
+        conv(5 + i)
+    rings[1].start(1)
+    rings[1].pass_on()
     rings[0].finish_recv()
-    ready(0)
-    unit(0, 0)
-    unit(1, 0)
-    spread(5)
-    share(1)
-    share(2)
-    spread(6)
-    spread(7)
-    ready(1)
-    ready(2)
-    unit(0, 1)
-    unit(1, 1)
-    share(3)
-    share(4)
-    rings[1].pass_on()
-    ready(3)
-    ready(4)
-    unit(0, 2)
-    unit(1, 2)
-    rings[1].finish_recv()
-    unit(2, 0)
-    unit(3, 0)
-    share(5)
-    share(6)
-    unit(2, 1)
-    unit(3, 1)
-    ready(5)
-    ready(6)
-    unit(0, 3)
-    unit(1, 3)
+    before = {0: ((), (0,)), 1: ((3, 4), (1, 2)), 4: ((5, 6, 7), (3, 4)), 8: ((), (5, 6))}
+    for i, (h, step) in enumerate(CHAINS):
+        if i == 3:
+            rings[1].finish_recv()
+        spreads, shares = before.get(i, ((), ()))
+        for k in spreads:
+            spread(k)
+        for k in shares:
+            share(k)
+        for k in shares:
+            ready(k)
+        ring_send(h, step)
     share(7)
-    unit(2, 2)
-    unit(3, 2)
     ready(7)
-    unit(2, 3)
-    unit(3, 3)
-    for h in range(4):
-        unit(h, 4)
+    ring_end()
 
     @pl.loop(0, NS)
     def _(i):
-        here, src, dst, to = piece(i)
-
-        @pl.when(jnp.logical_not(here))
-        def _():
-            remote(src, dst, ssem.at[i], rsem, to).wait_send()
+        posted(i, tx, rx, ssem, rsem)
 
     @pl.loop(0, 8)
     def _(i):
@@ -491,8 +475,8 @@
         ((256, 1024), bf16),
         ((256, 384), f32),
         ((4, 256, 256), bf16),
-        ((NS, MSG, BLK), bf16),
-        ((NS, MSG, BLK), bf16),
+        ((NS, 48, BLK), bf16),
+        ((NS, 48, BLK), bf16),
         ((8, BLK, BLK), bf16),
         ((8, BLK, BLK), bf16),
         ((DB, CH, 2 * BLK), bf16),
@@ -502,21 +486,21 @@
         ((NY, CH, 2 * BLK), f32),
         ((REC, CH, 2 * BLK), f32),
         ((NZ, NY, CH, BLK), bf16),
-        ((NY, 1024, 256), bf16),
+        ((1024, 1024), bf16),
         ((NZ, NX, 2, BLK, BLK), bf16),
         ((2, 4, 4, 256, BLK), bf16),
         ((2, 4, 4, 256, BLK), bf16),
     ]
     semaphores = [
-        dma((6,)), dma((NS,)), dma, dma((8,)), dma, dma, dma((NZ, NY)), dma((NZ,)), dma((NZ, NX)), dma((NZ, NX)),
+        dma((7,)), dma((NS,)), dma, dma((8,)), dma, dma, dma((NZ, NY)), dma((NZ,)), dma((NZ, NX)), dma((NZ, NX)),
         dma((NZ,)), dma((NZ,)), dma((6,)), dma((6,)), dma((6,)), dma((6,)), dma((2, 4, 4)), dma((2, 4, 4)),
     ]
     return pl.pallas_call(
         hyena_kernel,
         out_shape=jax.ShapeDtypeStruct((BLK, 1024), bf16),
-        in_specs=[pl.BlockSpec(memory_space=pltpu.SMEM)] + [hbm] * 6,
+        in_specs=[hbm] * 7,
         out_specs=vm,
-        scratch_shapes=[pltpu.VMEM(*s) for s in scratch] + [pltpu.SMEM((3, NS), jnp.int32)] + semaphores,
+        scratch_shapes=[pltpu.VMEM(*s) for s in scratch] + [pltpu.SMEM((3, NS), jnp.int32), pltpu.SMEM((REC,), jnp.int32)] + semaphores,
         compiler_params=pltpu.CompilerParams(collective_id=0, has_side_effects=True, vmem_limit_bytes=60 << 20),
         name="hyena",
     )(lengths, q, k, v, taps.T, weight, jnp.asarray(dft_tables()))

time: 75.6 us -> 68.5 us (0.906)
  the two profiles are of different devices: /device:TPU:8 before, /device:TPU:1 now
where the time goes in v3:
time: 68.5 us; the launch traced here: 68.4 us
  Pallas kernels  66.7 us (97%)
  local copies, waits for them, and re-layouts  1.67 us (2%)
    pallas_call x1, Pallas kernels, shards(): pl.pallas_call(hyena_kernel, out_shape=jax.ShapeDtypeStruct((BLK, 1024),...  66.7 us
    unnamed x1, local copies, waits for them, and re-layouts  1.67 us

profile of v3, /device:TPU:1, one launch (start us, length us, event | category | flops | bytes accessed | tf_op | source)
XLA Modules:
  0.0 68.4 jit_solution(11282167889780707109)
XLA Ops:
  0.0 66.7 %hyena.1 = bf16[128,1024]{1,0:T(8,128)(2,1)} custom-call(s32[8]{0:T(128)} %len_hbm.1, bf16[128,1024]{1,0:T(8,128)(2,1)} %q_hbm.1, bf16[128,1024]{1,0:T(8,128)(2,1)} %k_hbm.1, bf16[128,1024]{1,0:T(8,128)(2,1)} %v_hbm.1, f32[64,1024]{1,0:T(8,128)} %bitcast.1, bf16[256,1024]{1,0:T(8,128)(2,1)} %w_hbm.1, f32[256,384]{1,0:T(8,128)} %constant.2.clone.tab_hbm), custom_call_target="tpu_custom_call" | custom-call | tf_op jit(solution)/shard_map/hyena/pallas_call | solution.py:498
  66.7 1.7 %copy.9 = bf16[128,1024]{1,0:T(8,128)(2,1)} copy(bf16[128,1024]{1,0:T(8,128)(2,1)} %hyena.1) | data formatting | bytes 524288

commit v4 on v3

--- a/solution.py
+++ b/solution.py
@@ -17,7 +17,8 @@
 f32 = jnp.float32
 ORDER = [4, 3, 5, 2, 6, 1, 7, 0]
 FAR = [2, 1, 3]
-CHAINS = [(0, 0), (1, 1), (0, 1), (2, 0), (1, 2), (3, 1), (0, 2), (2, 1), (1, 3), (3, 2), (2, 2), (0, 3), (3, 3), (2, 3)]
+CHAINS = [(0, 0), (1, 1), (0, 1), (2, 0), (3, 1), (1, 2), (0, 2), (2, 1), (1, 3), (3, 2), (2, 2), (0, 3), (3, 3), (2, 3)]
+FARZ = ["3210", "3210", "2130", "1023", "0123", "0123", "0132", "3021"]
 
 
 def coords():
@@ -91,11 +92,29 @@
 
 def hyena_kernel(
     len_hbm, q_hbm, k_hbm, v_hbm, t_hbm, w_hbm, tab_hbm, out,
-    q_ref, k_ref, v_ref, t_ref, w_ref, tab_ref, tab, tx, rx, qt, qall, hcat, xrow, xh, gh, yh, ye, cv, wt, gall, sbuf, rbuf, seg, len_ref,
+    q_ref, k_ref, v_ref, t_ref, w_ref, tab_ref, tab, tx, rx, qt, qall, hcat, xrow, xh, gh, yh, ye, cv, wt, gall, sbuf, rbuf, result, seg, len_ref,
     isem, ssem, rsem, qsend, qrecv, nsem, asend, arecv, bsend, brecv, csend, crecv, w0send, w0recv, w1send, w1recv,
-    zsend, zrecv,
+    zsend, zrecv, osem,
 ):
     x, core, y, z = coords()
+    own = (z // 4 == core).astype(jnp.int32)
+    mate = dev(x, 1 - core, y, z)
+    ys = [dev(x, core, (y + i) % NY, z) for i in FAR]
+    xs = [dev((x + i) % NX, core, y, z) for i in FAR]
+    zs = [dev(x, core, y, (z + 1) % NZ), dev(x, core, y, (z + NZ - 1) % NZ)]
+    barrier = pltpu.get_barrier_semaphore()
+
+    @pl.loop(0, NS)
+    def _(i):
+        far = dev(x, z // 4, (y + 2 + i // NZ) % NY, (z + 4 + i % NZ) % NZ)
+
+        @pl.when(jnp.logical_not((own == 1) & (i == 2 * NZ + 4)))
+        def _():
+            signal(barrier, far)
+
+    for d in ys + xs + zs + [mate]:
+        signal(barrier, d)
+
     loads = [
         pltpu.make_async_copy(src, dst, isem.at[i])
         for i, (src, dst) in enumerate(
@@ -105,21 +124,15 @@
     for c in loads:
         c.start()
 
-    own = (z // 4 == core).astype(jnp.int32)
-    mate = dev(x, 1 - core, y, z)
-    ys = [dev(x, core, (y + i) % NY, z) for i in FAR]
-    xs = [dev((x + i) % NX, core, y, z) for i in FAR]
-    zs = [dev(x, core, y, (z + 1) % NZ), dev(x, core, y, (z + NZ - 1) % NZ)]
-    barrier = pltpu.get_barrier_semaphore()
-    for d in ys + xs + zs + [mate]:
-        signal(barrier, d)
-
-    @pl.loop(0, NS)
-    def _(i):
-        @pl.when(jnp.logical_not((own == 1) & (i == y * NZ + z)))
-        def _():
-            signal(barrier, (i, x * 2 + z // 4))
-
+    def flip(a):
+        return a.T
+
+    loads[0].wait()
+    loads[1].wait()
+    for c in range(8):
+        cols = pl.ds(c * BLK, BLK)
+        prod = (k_ref[:, cols].astype(f32) * v_ref[:, cols].astype(f32)).astype(bf16)
+        tx[pl.ds(4 * c, 4), pl.ds(0, CH), :] = flip(prod).reshape(4, CH, BLK)
     loads[2].wait()
     for c in range(8):
         taps = t_ref[:, pl.ds(c * BLK, BLK)].T.reshape(4, CH, 64)
@@ -156,50 +169,52 @@
         def _():
             remote(src.at[p], dst.at[y * NZ + z], send.at[i], recv, to).wait_send()
 
-    for c in loads[:2]:
-        c.wait()
-
-    @pl.loop(0, 8)
+    @pl.loop(0, NS)
     def _(i):
-        c = chunk(i)
-        cols = pl.ds(pl.multiple_of(c * BLK, BLK), BLK)
-        prod = (k_ref[:, cols].astype(f32) * v_ref[:, cols].astype(f32)).T
-        tx[pl.ds(4 * c, 4), pl.ds(0, CH), :] = prod.astype(bf16).reshape(4, CH, BLK)
-        for j in range(NY):
-            post(4 * i + j, tx, rx, ssem, rsem)
+        post(i, tx, rx, ssem, rsem)
 
     loads[3].wait()
     w_cols = pl.ds(pl.multiple_of(y * 256, 256), 256)
     for c in range(4):
-        wt[pl.ds(c * BLK, BLK), w_cols] = w_ref[:, pl.ds(c * BLK, BLK)].astype(f32).T.astype(bf16)
+        wt[pl.ds(c * BLK, BLK), w_cols] = flip(w_ref[:, pl.ds(c * BLK, BLK)])
     rings = [Ring(wt, 0, w0send, w0recv, x, core, y, z), Ring(wt, 512, w1send, w1recv, x, core, y, z)]
     rings[0].start(0)
     rings[0].start(1)
 
     loads[4].wait()
     for c in range(8):
-        qt[c] = q_ref[:, pl.ds(c * BLK, BLK)].astype(f32).T.astype(bf16)
+        qt[c] = flip(q_ref[:, pl.ds(c * BLK, BLK)])
+
+    farz = jnp.int32(0)
+    for i, digits in enumerate(FARZ):
+        farz = jnp.where((4 * core + 8 - z) % 8 == i, int(digits[::-1], 4), farz)
 
     def q_piece(i):
-        p = (i + 2 * (z % 4) + core) % 8
+        digit = farz
+        for k in range(1, 4):
+            digit = jnp.where(i // 2 == k, farz // 4**k, digit)
+        p = 2 * (digit % 4) + (i + core) % 2
         to = dev(x, p % 2, y, 4 * core + p // 2)
-        here = (own == 1) & (i == 0)
+        here = (own == 1) & (p == 2 * (z % 4) + core)
         return here, qt.at[p], qall.at[z], to
 
-    @pl.loop(0, 8)
-    def _(i):
-        here, src, dst, to = q_piece(i)
-
-        @pl.when(here)
-        def _():
-            pltpu.make_async_copy(src, dst, qrecv).start()
-
-        @pl.when(jnp.logical_not(here))
-        def _():
-            remote(src, dst, qsend.at[i], qrecv, to).start()
+    def q_post(low, high):
+        @pl.loop(low, high)
+        def _(i):
+            here, src, dst, to = q_piece(i)
+
+            @pl.when(here)
+            def _():
+                pltpu.make_async_copy(src, dst, qrecv.at[z]).start()
+
+            @pl.when(jnp.logical_not(here))
+            def _():
+                remote(src, dst, qsend.at[i], qrecv.at[z], to).start()
+
+    q_post(0, 2)
 
     for c in range(4):
-        wt[pl.ds(512 + c * BLK, BLK), w_cols] = w_ref[:, pl.ds(512 + c * BLK, BLK)].astype(f32).T.astype(bf16)
+        wt[pl.ds(512 + c * BLK, BLK), w_cols] = flip(w_ref[:, pl.ds(512 + c * BLK, BLK)])
 
     loads[6].wait()
     bounds = []
@@ -235,6 +250,7 @@
     rings[0].pass_on()
     rings[1].start(0)
     pltpu.make_async_copy(tx, rx, rsem).wait()
+    q_post(2, 8)
 
     lane16 = lax.broadcasted_iota(jnp.int32, (16, BLK), 1)
     lane = lax.broadcasted_iota(jnp.int32, (CH, BLK), 1)
@@ -242,7 +258,7 @@
     hcat[0, :, pl.ds(BLK, BLK)] = zero
     hcat[DB - 1, :, pl.ds(0, BLK)] = zero
 
-    @pl.loop(0, DB - 1)
+    @pl.loop(0, DB - 1, unroll=4)
     def _(d):
         a = rx[2 * d, pl.ds(CH, 16), :].astype(f32)
         b = rx[2 * d + 1, pl.ds(CH, 16), :].astype(f32)
@@ -256,7 +272,7 @@
         taps = hcat[pl.ds(lo, size)].reshape(size * CH, 2 * BLK)
         gh[pl.ds(lo, size)] = (dot(taps, tab[0]) + dot(taps, tab[1])).reshape(size, CH, 2 * BLK)
 
-    @pl.loop(0, NS)
+    @pl.loop(0, NS, unroll=8)
     def _(n):
         row = rx[n, pl.ds(0, CH), :].astype(f32)
         xrow[n] = jnp.where(lane + n * BLK < seg[1, n], row, 0.0).astype(bf16)
@@ -296,7 +312,7 @@
     def convolve(rel):
         b = place(rel)
 
-        @pl.loop(0, NY)
+        @pl.loop(0, NY, unroll=2)
         def _(j):
             n = j * NZ + b
             block, first = seg[0, n], seg[2, n]
@@ -355,6 +371,7 @@
         b = place(rel)
         ref = gall.at[b, x, core]
         pltpu.make_async_copy(ref, ref, arecv.at[rel]).wait()
+        pltpu.make_async_copy(qall.at[b], qall.at[b], qrecv.at[b]).wait()
         gall[b, x, core] = (gall[b, x, core].astype(f32) * qall[b].astype(f32)).astype(bf16)
         for c in b_copies(rel):
             c.start()
@@ -392,6 +409,9 @@
             sbuf[way, k, step] = total.astype(bf16)
             z_copy(way, k, step).start()
 
+    def store(h):
+        return pltpu.make_async_copy(result.at[:, rows(h)], out.at[:, rows(h)], osem.at[h])
+
     def ring_end():
         terms = [term(h, 0) for h in range(4)]
         for h in (0, 1, 2, 3):
@@ -399,30 +419,39 @@
             for way in range(2):
                 z_copy(way, h, 3).wait_recv()
                 total = total + rbuf[way, h, 3].astype(f32)
-            out[:, rows(h)] = total.T.astype(bf16)
+            result[:, rows(h)] = total.T.astype(bf16)
+            store(h).start()
 
     for i in range(5):
         conv(i)
-    pltpu.make_async_copy(qt, qall, qrecv).wait()
+        if i == 2:
+            rings[1].start(1)
     for i in range(3):
         spread(i)
         conv(5 + i)
-    rings[1].start(1)
     rings[1].pass_on()
     rings[0].finish_recv()
-    before = {0: ((), (0,)), 1: ((3, 4), (1, 2)), 4: ((5, 6, 7), (3, 4)), 8: ((), (5, 6))}
+    before = {
+        0: ((), (0,), (0,)),
+        1: ((3, 4), (1, 2), (1, 2)),
+        2: ((5, 6), (), ()),
+        4: ((7,), (3, 4), ()),
+        5: ((), (), (3, 4)),
+        7: ((), (5, 6), ()),
+        8: ((), (), (5, 6)),
+        11: ((), (7,), ()),
+    }
     for i, (h, step) in enumerate(CHAINS):
         if i == 3:
             rings[1].finish_recv()
-        spreads, shares = before.get(i, ((), ()))
+        spreads, shares, needs = before.get(i, ((), (), ()))
         for k in spreads:
             spread(k)
         for k in shares:
             share(k)
-        for k in shares:
+        for k in needs:
             ready(k)
         ring_send(h, step)
-    share(7)
     ready(7)
     ring_end()
 
@@ -436,7 +465,7 @@
 
         @pl.when(jnp.logical_not(here))
         def _():
-            remote(src, dst, qsend.at[i], qrecv, to).wait_send()
+            remote(src, dst, qsend.at[i], qrecv.at[z], to).wait_send()
 
     for rel in range(NZ):
         for c in a_far(rel) + b_copies(rel) + [c_copy(rel)]:
@@ -448,6 +477,8 @@
                     z_copy(way, h, step).wait_send()
     for ring in rings:
         ring.finish_send()
+    for h in range(4):
+        store(h).wait()
 
 
 TOKENS_END = NS * BLK
@@ -464,7 +495,6 @@
 
 
 def shards(q, k, v, taps, weight, lengths):
-    vm = pl.BlockSpec(memory_space=pltpu.VMEM)
     hbm = pl.BlockSpec(memory_space=pl.ANY)
     dma = pltpu.SemaphoreType.DMA
     scratch = [
@@ -490,16 +520,17 @@
         ((NZ, NX, 2, BLK, BLK), bf16),
         ((2, 4, 4, 256, BLK), bf16),
         ((2, 4, 4, 256, BLK), bf16),
+        ((BLK, 1024), bf16),
     ]
     semaphores = [
-        dma((7,)), dma((NS,)), dma, dma((8,)), dma, dma, dma((NZ, NY)), dma((NZ,)), dma((NZ, NX)), dma((NZ, NX)),
-        dma((NZ,)), dma((NZ,)), dma((6,)), dma((6,)), dma((6,)), dma((6,)), dma((2, 4, 4)), dma((2, 4, 4)),
+        dma((7,)), dma((NS,)), dma, dma((8,)), dma((NZ,)), dma, dma((NZ, NY)), dma((NZ,)), dma((NZ, NX)), dma((NZ, NX)),
+        dma((NZ,)), dma((NZ,)), dma((6,)), dma((6,)), dma((6,)), dma((6,)), dma((2, 4, 4)), dma((2, 4, 4)), dma((4,)),
     ]
     return pl.pallas_call(
         hyena_kernel,
         out_shape=jax.ShapeDtypeStruct((BLK, 1024), bf16),
         in_specs=[hbm] * 7,
-        out_specs=vm,
+        out_specs=hbm,
         scratch_shapes=[pltpu.VMEM(*s) for s in scratch] + [pltpu.SMEM((3, NS), jnp.int32), pltpu.SMEM((REC,), jnp.int32)] + semaphores,
         compiler_params=pltpu.CompilerParams(collective_id=0, has_side_effects=True, vmem_limit_bytes=60 << 20),
         name="hyena",

time: 68.5 us -> 65.7 us (0.959)
  Pallas kernels: 66.7 us -> 63.9 us
    pallas_call x1, Pallas kernels: 66.7 us -> 63.9 us  [shards(): pl.pallas_call(hyena_kernel, out_shape=jax.ShapeDtypeStruct((BLK, 1024),...]
where the time goes in v4:
time: 65.7 us; the launch traced here: 65.6 us
  Pallas kernels  63.9 us (97%)
  local copies, waits for them, and re-layouts  1.67 us (3%)
    pallas_call x1, Pallas kernels, shards(): pl.pallas_call(hyena_kernel, out_shape=jax.ShapeDtypeStruct((BLK, 1024),...  63.9 us
    unnamed x1, local copies, waits for them, and re-layouts  1.67 us

profile of v4, /device:TPU:1, one launch (start us, length us, event | category | flops | bytes accessed | tf_op | source)
XLA Modules:
  0.0 65.6 jit_solution(271943518275951734)
XLA Ops:
  0.0 63.9 %hyena.1 = bf16[128,1024]{1,0:T(8,128)(2,1)} custom-call(s32[8]{0:T(128)} %len_hbm.1, bf16[128,1024]{1,0:T(8,128)(2,1)} %q_hbm.1, bf16[128,1024]{1,0:T(8,128)(2,1)} %k_hbm.1, bf16[128,1024]{1,0:T(8,128)(2,1)} %v_hbm.1, f32[64,1024]{1,0:T(8,128)} %bitcast.1, bf16[256,1024]{1,0:T(8,128)(2,1)} %w_hbm.1, f32[256,384]{1,0:T(8,128)} %constant.2.clone.tab_hbm), custom_call_target="tpu_custom_call" | custom-call | tf_op jit(solution)/shard_map/hyena/pallas_call | solution.py:529
  64.0 1.7 %copy.9 = bf16[128,1024]{1,0:T(8,128)(2,1)} copy(bf16[128,1024]{1,0:T(8,128)(2,1)} %hyena.1) | data formatting | bytes 524288

commit v5 on v4

--- a/solution.py
+++ b/solution.py
@@ -92,7 +92,7 @@
 
 def hyena_kernel(
     len_hbm, q_hbm, k_hbm, v_hbm, t_hbm, w_hbm, tab_hbm, out,
-    q_ref, k_ref, v_ref, t_ref, w_ref, tab_ref, tab, tx, rx, qt, qall, hcat, xrow, xh, gh, yh, ye, cv, wt, gall, sbuf, rbuf, result, seg, len_ref,
+    q_ref, k_ref, v_ref, t_ref, w_ref, tab_ref, tab, tx, rx, qt, qall, hcat, xh, gh, yh, ye, cv, wt, gall, sbuf, rbuf, result, seg, len_ref,
     isem, ssem, rsem, qsend, qrecv, nsem, asend, arecv, bsend, brecv, csend, crecv, w0send, w0recv, w1send, w1recv,
     zsend, zrecv, osem,
 ):
@@ -258,8 +258,7 @@
     hcat[0, :, pl.ds(BLK, BLK)] = zero
     hcat[DB - 1, :, pl.ds(0, BLK)] = zero
 
-    @pl.loop(0, DB - 1, unroll=4)
-    def _(d):
+    for d in range(DB - 1):
         a = rx[2 * d, pl.ds(CH, 16), :].astype(f32)
         b = rx[2 * d + 1, pl.ds(CH, 16), :].astype(f32)
         top = jnp.where(lane16 < 64, a, pltpu.roll(b, 64, 1))
@@ -268,28 +267,26 @@
         hcat[d, :, pl.ds(0, BLK)] = h
         hcat[d + 1, :, pl.ds(BLK, BLK)] = h
 
+    def row(n):
+        if n < NS:
+            value = rx[n, pl.ds(0, CH), :].astype(f32)
+            return jnp.where(lane + n * BLK < seg[1, n], value, 0.0).astype(bf16)
+        if n == NS:
+            return zero
+        begin, end = bounds[n - NS]
+        m = begin // BLK
+        token = lane + m * BLK
+        value = rx[m, pl.ds(0, CH), :].astype(f32)
+        return jnp.where((token >= begin) & (token < end), value, 0.0).astype(bf16)
+
+    for g in range(5):
+        rows = jnp.concatenate([row(8 * g + n) for n in range(8)], axis=0)
+        spectrum = dot(jnp.concatenate([rows, rows], axis=1), tab[2])
+        xh[pl.ds(8 * g, 8)] = spectrum.reshape(8, CH, 2 * BLK)
+
     for lo, size in ((0, 8), (8, 9)):
         taps = hcat[pl.ds(lo, size)].reshape(size * CH, 2 * BLK)
         gh[pl.ds(lo, size)] = (dot(taps, tab[0]) + dot(taps, tab[1])).reshape(size, CH, 2 * BLK)
-
-    @pl.loop(0, NS, unroll=8)
-    def _(n):
-        row = rx[n, pl.ds(0, CH), :].astype(f32)
-        xrow[n] = jnp.where(lane + n * BLK < seg[1, n], row, 0.0).astype(bf16)
-
-    xrow[NS] = zero
-    for r in range(1, REC):
-        begin, end = bounds[r]
-        n = begin // BLK
-        token = lane + n * BLK
-        row = rx[n, pl.ds(0, CH), :].astype(f32)
-        xrow[NS + r] = jnp.where((token >= begin) & (token < end), row, 0.0).astype(bf16)
-
-    @pl.loop(0, 5)
-    def _(g):
-        rows = xrow[pl.ds(8 * g, 8)].reshape(8 * CH, BLK)
-        spectrum = dot(jnp.concatenate([rows, rows], axis=1), tab[2])
-        xh[pl.ds(8 * g, 8)] = spectrum.reshape(8, CH, 2 * BLK)
 
     re, im = pl.ds(0, BLK), pl.ds(BLK, BLK)
 
@@ -312,7 +309,7 @@
     def convolve(rel):
         b = place(rel)
 
-        @pl.loop(0, NY, unroll=2)
+        @pl.loop(0, NY, unroll=4)
         def _(j):
             n = j * NZ + b
             block, first = seg[0, n], seg[2, n]
@@ -422,13 +419,14 @@
             result[:, rows(h)] = total.T.astype(bf16)
             store(h).start()
 
-    for i in range(5):
+    for i in range(4):
         conv(i)
         if i == 2:
             rings[1].start(1)
-    for i in range(3):
-        spread(i)
-        conv(5 + i)
+    for i in range(4):
+        if i < 3:
+            spread(i)
+        conv(4 + i)
     rings[1].pass_on()
     rings[0].finish_recv()
     before = {
@@ -510,7 +508,6 @@
         ((8, BLK, BLK), bf16),
         ((8, BLK, BLK), bf16),
         ((DB, CH, 2 * BLK), bf16),
-        ((NS + REC, CH, BLK), bf16),
         ((NS + REC, CH, 2 * BLK), f32),
         ((DB, CH, 2 * BLK), f32),
         ((NY, CH, 2 * BLK), f32),

time: 65.7 us -> 64.1 us (0.976)
  Pallas kernels: 63.9 us -> 62.3 us
    pallas_call x1, Pallas kernels: 63.9 us -> 62.3 us  [shards(): pl.pallas_call(hyena_kernel, out_shape=jax.ShapeDtypeStruct((BLK, 1024),...]
where the time goes in v5:
time: 64.1 us; the launch traced here: 64 us
  Pallas kernels  62.3 us (97%)
  local copies, waits for them, and re-layouts  1.67 us (3%)
    pallas_call x1, Pallas kernels, shards(): pl.pallas_call(hyena_kernel, out_shape=jax.ShapeDtypeStruct((BLK, 1024),...  62.3 us
    unnamed x1, local copies, waits for them, and re-layouts  1.67 us

profile of v5, /device:TPU:1, one launch (start us, length us, event | category | flops | bytes accessed | tf_op | source)
XLA Modules:
  0.0 64.0 jit_solution(17616511932146794830)
XLA Ops:
  0.0 62.3 %hyena.1 = bf16[128,1024]{1,0:T(8,128)(2,1)} custom-call(s32[8]{0:T(128)} %len_hbm.1, bf16[128,1024]{1,0:T(8,128)(2,1)} %q_hbm.1, bf16[128,1024]{1,0:T(8,128)(2,1)} %k_hbm.1, bf16[128,1024]{1,0:T(8,128)(2,1)} %v_hbm.1, f32[64,1024]{1,0:T(8,128)} %bitcast.1, bf16[256,1024]{1,0:T(8,128)(2,1)} %w_hbm.1, f32[256,384]{1,0:T(8,128)} %constant.2.clone.tab_hbm), custom_call_target="tpu_custom_call" | custom-call | tf_op jit(solution)/shard_map/hyena/pallas_call | solution.py:526
  62.3 1.7 %copy.9 = bf16[128,1024]{1,0:T(8,128)(2,1)} copy(bf16[128,1024]{1,0:T(8,128)(2,1)} %hyena.1) | data formatting | bytes 524288

commit v6 on v5

--- a/solution.py
+++ b/solution.py
@@ -173,18 +173,9 @@
     def _(i):
         post(i, tx, rx, ssem, rsem)
 
-    loads[3].wait()
-    w_cols = pl.ds(pl.multiple_of(y * 256, 256), 256)
-    for c in range(4):
-        wt[pl.ds(c * BLK, BLK), w_cols] = flip(w_ref[:, pl.ds(c * BLK, BLK)])
-    rings = [Ring(wt, 0, w0send, w0recv, x, core, y, z), Ring(wt, 512, w1send, w1recv, x, core, y, z)]
-    rings[0].start(0)
-    rings[0].start(1)
-
     loads[4].wait()
     for c in range(8):
         qt[c] = flip(q_ref[:, pl.ds(c * BLK, BLK)])
-
     farz = jnp.int32(0)
     for i, digits in enumerate(FARZ):
         farz = jnp.where((4 * core + 8 - z) % 8 == i, int(digits[::-1], 4), farz)
@@ -212,6 +203,15 @@
                 remote(src, dst, qsend.at[i], qrecv.at[z], to).start()
 
     q_post(0, 2)
+
+    loads[3].wait()
+    w_cols = pl.ds(pl.multiple_of(y * 256, 256), 256)
+    for c in range(4):
+        wt[pl.ds(c * BLK, BLK), w_cols] = flip(w_ref[:, pl.ds(c * BLK, BLK)])
+    rings = [Ring(wt, 0, w0send, w0recv, x, core, y, z), Ring(wt, 512, w1send, w1recv, x, core, y, z)]
+    rings[0].start(0)
+    rings[0].start(1)
+
 
     for c in range(4):
         wt[pl.ds(512 + c * BLK, BLK), w_cols] = flip(w_ref[:, pl.ds(512 + c * BLK, BLK)])
@@ -431,8 +431,9 @@
     rings[0].finish_recv()
     before = {
         0: ((), (0,), (0,)),
-        1: ((3, 4), (1, 2), (1, 2)),
-        2: ((5, 6), (), ()),
+        1: ((3,), (1, 2), (1, 2)),
+        2: ((4, 5), (), ()),
+        3: ((6,), (), ()),
         4: ((7,), (3, 4), ()),
         5: ((), (), (3, 4)),
         7: ((), (5, 6), ()),

time: 64.1 us -> 64 us (level)
  no operation moved by 1% of the time
where the time goes in v6:
time: 64 us; the launch traced here: 63.9 us
  Pallas kernels  62.2 us (97%)
  local copies, waits for them, and re-layouts  1.67 us (3%)
    pallas_call x1, Pallas kernels, shards(): pl.pallas_call(hyena_kernel, out_shape=jax.ShapeDtypeStruct((BLK, 1024),...  62.2 us
    unnamed x1, local copies, waits for them, and re-layouts  1.67 us

profile of v6, /device:TPU:1, one launch (start us, length us, event | category | flops | bytes accessed | tf_op | source)
XLA Modules:
  0.0 63.9 jit_solution(3330502723362218410)
XLA Ops:
  0.0 62.2 %hyena.1 = bf16[128,1024]{1,0:T(8,128)(2,1)} custom-call(s32[8]{0:T(128)} %len_hbm.1, bf16[128,1024]{1,0:T(8,128)(2,1)} %q_hbm.1, bf16[128,1024]{1,0:T(8,128)(2,1)} %k_hbm.1, bf16[128,1024]{1,0:T(8,128)(2,1)} %v_hbm.1, f32[64,1024]{1,0:T(8,128)} %bitcast.1, bf16[256,1024]{1,0:T(8,128)(2,1)} %w_hbm.1, f32[256,384]{1,0:T(8,128)} %constant.2.clone.tab_hbm), custom_call_target="tpu_custom_call" | custom-call | tf_op jit(solution)/shard_map/hyena/pallas_call | solution.py:527
  62.2 1.7 %copy.9 = bf16[128,1024]{1,0:T(8,128)(2,1)} copy(bf16[128,1024]{1,0:T(8,128)(2,1)} %hyena.1) | data formatting | bytes 524288

commit v7 on v6

--- a/solution.py
+++ b/solution.py
@@ -250,7 +250,6 @@
     rings[0].pass_on()
     rings[1].start(0)
     pltpu.make_async_copy(tx, rx, rsem).wait()
-    q_post(2, 8)
 
     lane16 = lax.broadcasted_iota(jnp.int32, (16, BLK), 1)
     lane = lax.broadcasted_iota(jnp.int32, (CH, BLK), 1)
@@ -421,6 +420,8 @@
 
     for i in range(4):
         conv(i)
+        if i == 0:
+            q_post(2, 8)
         if i == 2:
             rings[1].start(1)
     for i in range(4):

time: 64 us -> 63.9 us (level)
  no operation moved by 1% of the time
where the time goes in v7:
time: 63.9 us; the launch traced here: 63.8 us
  Pallas kernels  62.1 us (97%)
  local copies, waits for them, and re-layouts  1.67 us (3%)
    pallas_call x1, Pallas kernels, shards(): pl.pallas_call(hyena_kernel, out_shape=jax.ShapeDtypeStruct((BLK, 1024),...  62.1 us
    unnamed x1, local copies, waits for them, and re-layouts  1.67 us

profile of v7, /device:TPU:1, one launch (start us, length us, event | category | flops | bytes accessed | tf_op | source)
XLA Modules:
  0.0 63.8 jit_solution(17646730765946450064)
XLA Ops:
  0.0 62.1 %hyena.1 = bf16[128,1024]{1,0:T(8,128)(2,1)} custom-call(s32[8]{0:T(128)} %len_hbm.1, bf16[128,1024]{1,0:T(8,128)(2,1)} %q_hbm.1, bf16[128,1024]{1,0:T(8,128)(2,1)} %k_hbm.1, bf16[128,1024]{1,0:T(8,128)(2,1)} %v_hbm.1, f32[64,1024]{1,0:T(8,128)} %bitcast.1, bf16[256,1024]{1,0:T(8,128)(2,1)} %w_hbm.1, f32[256,384]{1,0:T(8,128)} %constant.2.clone.tab_hbm), custom_call_target="tpu_custom_call" | custom-call | tf_op jit(solution)/shard_map/hyena/pallas_call | solution.py:528
  62.1 1.7 %copy.9 = bf16[128,1024]{1,0:T(8,128)(2,1)} copy(bf16[128,1024]{1,0:T(8,128)(2,1)} %hyena.1) | data formatting | bytes 524288
